TPU v7x, 128 devices: a whole 4x4x4 slice. The times are simulated.
128 devices in a mesh: sec: 4 (over y_hi, core), tile: 32 (over z, x, y_lo).
Axes of the slice: x: 4, y: 4 (y_hi: 2, y_lo: 2; y = y_hi * 2 + y_lo), z: 4, core: 2. Of those that a mesh axis runs over, the one named last changes fastest.
Arguments:
- fields: float32 [4, 4, 2048, 256], P('sec', None, 'tile'), may hold values from -6 to 6
- coefficients: float32 [4, 2, 2048, 256], P('sec', None, 'tile'), may hold values from 0.04 to 0.24
- owner_tile: int32 [6144, 2], replicated, may hold values from 0 to 31, all different within a row; in each aligned block of 64 rows (0 to 63, 64 to 127, ...) at most 8 rows name the same one
- dest_block: int32 [6144, 2], replicated, may hold values from 0 to 63
- table_index: int32 [6144, 2], replicated, may hold values from 0 to 3
- tables: float32 [4, 256, 256], replicated, may hold values from -0.375 to 0.375
- land_mask: int32 [2048, 256], P('tile'), may hold values 0 or 1
Outputs:
- fields_out: float32 [4, 4, 2048, 256], P('sec', None, 'tile')
- surface: float32 [4, 2048, 256], P('sec', 'tile')
Inputs may be any that keep to these rules, and one draw needn't show every extreme that they name: `owner_tile`: each row names 2 different ocean tiles; in each aligned block of 64 rows (the blocks of one atmosphere device) no tile is named more than 8 times.
All inputs are finite; a program needn't handle non-finite values. No bound on the sum of `land_mask` on one device may be relied on, other than what follows from the above.
Results may differ from a plain program's by a relative error of at most 0.0001.
Values sent between devices are 32-bit elements; how exact they have to be, the bound alone decides.
A program may use at most 64 MiB of HBM per device.

v0:
```python
import jax
import jax.numpy as jnp
from jax import lax
from jax.sharding import PartitionSpec as P

STENCIL_SUBSTEPS = 2


forcing_rate = 0.5


def with_halo(shard, sides, width):
    for axis, dim in sides:
        size, length = (lax.axis_size(axis), shard.shape[dim])
        up = [(i, (i + 1) % size) for i in range(size - 1)]
        down = [(j, i) for i, j in up]
        last = lax.slice_in_dim(shard, length - width, length, axis=dim)
        first = lax.slice_in_dim(shard, 0, width, axis=dim)
        before = lax.ppermute(last, axis, up)
        after = lax.ppermute(first, axis, down)
        shard = jnp.concatenate([before, shard, after], axis=dim)
    return shard


def advance(extended, kappa_rows, speed_rows):
    center = extended[:, 1:-1]
    upper_row = extended[:, :-2]
    lower_row = extended[:, 2:]
    laplace = (
        upper_row
        + lower_row
        + jnp.roll(center, 1, axis=2)
        + jnp.roll(center, -1, axis=2)
        - 4.0 * center
    )
    return center + kappa_rows * laplace - 0.5 * speed_rows * (lower_row - upper_row)


def local(fields, coefficients, owner_tile, dest_block, table_index, tables, land_mask):
    levels_here = fields[0]
    kappa = coefficients[0, 0]
    speed = coefficients[0, 1]
    rows = levels_here.shape[1]
    width = levels_here.shape[2]
    n_sec = lax.axis_size("sec")
    n_tile = lax.axis_size("tile")
    sec_index = lax.axis_index("sec")
    tile_index = lax.axis_index("tile")
    current = levels_here
    for _ in range(STENCIL_SUBSTEPS):
        extended = with_halo(current, (("tile", 1),), 1)
        current = advance(extended, kappa, speed)
    fan_out = owner_tile.shape[1]
    pairs_count = rows * fan_out
    cap = 2 * fan_out * rows // n_tile
    atm_count = (n_sec - 1) * n_tile
    table_total = tables.shape[0]
    source_section = jnp.minimum(sec_index, n_sec - 2)
    leading_row = (source_section * n_tile + tile_index) * rows
    my_owner = lax.dynamic_slice_in_dim(owner_tile, leading_row, rows, 0).reshape(-1)
    my_table = lax.dynamic_slice_in_dim(table_index, leading_row, rows, 0)
    tile_ids = jnp.arange(n_tile, dtype=jnp.int32)
    owner_hot = (my_owner[:, None] == tile_ids[None, :]).astype(jnp.int32)
    earlier = jnp.cumsum(owner_hot, axis=0) - owner_hot
    slot_of = jnp.sum(earlier * owner_hot, axis=1)
    target = my_owner * cap + slot_of
    placing = (target[None, :] == jnp.arange(n_tile * cap, dtype=jnp.int32)[:, None]).astype(
        jnp.float32
    )
    is_atmos = (sec_index < n_sec - 1).astype(jnp.float32)
    is_ocean = 1.0 - is_atmos
    message_values = jnp.stack([current[0], current[0] - current[1]], axis=1)
    pair_rows = jnp.broadcast_to(message_values[:, None], (rows, fan_out, 2, width))
    pair_rows = pair_rows.reshape(pairs_count, 2 * width) * is_atmos
    send_buffer = jnp.dot(placing, pair_rows, precision=lax.Precision.HIGHEST).reshape(
        n_tile, cap, 2, width
    )
    outgoing = jnp.concatenate(
        [jnp.zeros((atm_count, cap, 2, width), jnp.float32), send_buffer], axis=0
    )
    received = lax.all_to_all(outgoing, ("sec", "tile"), split_axis=0, concat_axis=0, tiled=True)
    from_atmos = received[:atm_count].reshape(atm_count * cap, 2, width)
    all_owner = owner_tile.reshape(atm_count, pairs_count)
    mine = (all_owner == tile_index).astype(jnp.int32)
    ranking = jnp.cumsum(mine, axis=1) - mine
    slot_ids = jnp.arange(cap, dtype=jnp.int32)
    slot_hot = mine[:, None, :] * (ranking[:, None, :] == slot_ids[None, :, None]).astype(jnp.int32)
    slot_dest = jnp.sum(slot_hot * dest_block.reshape(atm_count, 1, pairs_count), axis=2).reshape(
        -1
    )
    slot_lookup_table = jnp.sum(
        slot_hot * table_index.reshape(atm_count, 1, pairs_count), axis=2
    ).reshape(-1)
    slot_valid = jnp.sum(slot_hot, axis=2).reshape(-1)
    contrib = jnp.zeros_like(from_atmos)
    for table_ordinal in range(table_total):
        weighted_values = jnp.einsum(
            "sfc,cd->sfd", from_atmos, tables[table_ordinal], precision=lax.Precision.HIGHEST
        )
        chosen = (slot_lookup_table == table_ordinal).astype(jnp.float32)
        contrib = contrib + chosen[:, None, None] * weighted_values
    spread = (
        (slot_dest[None, :] == jnp.arange(rows, dtype=jnp.int32)[:, None])
        & (slot_valid[None, :] > 0)
    ).astype(jnp.float32)
    flux = jnp.dot(spread, contrib.reshape(-1, 2 * width), precision=lax.Precision.HIGHEST).reshape(
        rows, 2, width
    )
    water = land_mask.astype(jnp.float32)
    top_level = current[0] + forcing_rate * water * flux[:, 0]
    second_level = current[1] + forcing_rate * water * flux[:, 1]
    forced = jnp.concatenate([top_level[None], second_level[None], current[2:]], axis=0)
    sea_values = water * top_level
    returning = (
        jnp.dot(spread.T, sea_values, precision=lax.Precision.HIGHEST).reshape(
            atm_count, cap, width
        )
        * is_ocean
    )
    back_full = jnp.concatenate([returning, jnp.zeros((n_tile, cap, width), jnp.float32)], axis=0)
    arrived = lax.all_to_all(back_full, ("sec", "tile"), split_axis=0, concat_axis=0, tiled=True)[
        atm_count:
    ]
    pair_values = jnp.dot(
        placing.T, arrived.reshape(n_tile * cap, width), precision=lax.Precision.HIGHEST
    )
    flat_table = my_table.reshape(-1)
    atm_pairs = jnp.zeros((pairs_count, width), jnp.float32)
    for table_ordinal in range(table_total):
        mirrored = jnp.dot(pair_values, tables[table_ordinal].T, precision=lax.Precision.HIGHEST)
        chosen = (flat_table == table_ordinal).astype(jnp.float32)
        atm_pairs = atm_pairs + chosen[:, None] * mirrored
    atmosphere_surface_field = atm_pairs.reshape(rows, fan_out, width).sum(axis=1)
    ocean_here = sec_index == n_sec - 1
    surface = jnp.where(ocean_here, sea_values, atmosphere_surface_field)[None]
    fields_out = jnp.where(ocean_here, forced, current)[None]
    return (fields_out, surface)


def solution(mesh):
    placed = (
        P("sec", None, "tile", None),
        P("sec", None, "tile", None),
        P(),
        P(),
        P(),
        P(),
        P("tile", None),
    )
    return jax.shard_map(
        local,
        mesh=mesh,
        in_specs=placed,
        out_specs=(P("sec", None, "tile", None), P("sec", "tile", None)),
        check_vma=False,
    )
```

profile of v0, /device:TPU:1, one launch (start us, length us, event | category | flops | bytes accessed | tf_op | source)
XLA Modules:
  0.0 112.5 jit_solution(9517677848391190309)
XLA Ops:
  0.7 0.8 fusion.84
  1.5 4.0 %collective-permute-start = (f32[4,1,256]{2,1,0:T(1,128)S(1)}, f32[4,1,256]{2,1,0:T(1,128)S(1)}, u32[]{:S(2)}, u32[]{:S(2)}) collective-permute-start(f32[4,1,256]{2,1,0:T(1,128)S(1)} %get-tuple-element.15), channel_id=1, source_target_pairs={{0,1},{1,2},{2,3},{3,4},{4,5},{5,6},{6,7},{7,8},{8,9},{9,10},{10,1... | collective-permute-start | bytes 12296 | tf_op jit(solution)/shard_map/ppermute | solution.py:19
  5.5 1.3 %collective-permute-start.1 = (f32[4,1,256]{2,1,0:T(1,128)S(1)}, f32[4,1,256]{2,1,0:T(1,128)S(1)}, u32[]{:S(2)}, u32[]{:S(2)}) collective-permute-start(f32[4,1,256]{2,1,0:T(1,128)S(1)} %get-tuple-element.14), channel_id=1, source_target_pairs={{1,0},{2,1},{3,2},{4,3},{5,4},{6,5},{7,6},{8,7},{9,8},{10,9},{11,1... | collective-permute-start | bytes 12296 | tf_op jit(solution)/shard_map/ppermute | solution.py:20
  6.8 1.2 %fusion.85 = (f32[4,64,255]{2,1,0:T(8,128)S(1)}, f32[4,64,255]{2,1,0:T(8,128)S(1)}) fusion(f32[4,64,256]{2,1,0:T(8,128)} %bitcast.126), kind=kLoop, calls=%fused_computation.127 | loop fusion | bytes 1044480 | tf_op jit(solution)/shard_map/jit(_roll_static)/slice | solution.py:33
  8.0 1.1 fusion.86
  9.1 0.1 constant_dynamic-slice_fusion.1
  9.2 0.1 copy.38
  9.3 0.1 reshape.204
  9.4 0.1 fusion.78
  9.5 0.2 reduce_window_sum.23
  9.7 0.2 select_reduce_fusion.1
  9.9 0.2 fusion.36
  10.2 0.1 fusion.82
  10.3 4.0 %collective-permute-start.2 = (f32[4,1,256]{2,1,0:T(1,128)S(1)}, f32[4,1,256]{2,1,0:T(1,128)S(1)}, u32[]{:S(2)}, u32[]{:S(2)}) collective-permute-start(f32[4,1,256]{2,1,0:T(1,128)S(1)} %get-tuple-element.9), channel_id=1, source_target_pairs={{0,1},{1,2},{2,3},{3,4},{4,5},{5,6},{6,7},{7,8},{8,9},{9,10},{10,1... | collective-permute-start | bytes 12296 | tf_op jit(solution)/shard_map/ppermute | solution.py:19
  14.3 1.3 %collective-permute-start.3 = (f32[4,1,256]{2,1,0:T(1,128)S(1)}, f32[4,1,256]{2,1,0:T(1,128)S(1)}, u32[]{:S(2)}, u32[]{:S(2)}) collective-permute-start(f32[4,1,256]{2,1,0:T(1,128)S(1)} %get-tuple-element.8), channel_id=1, source_target_pairs={{1,0},{2,1},{3,2},{4,3},{5,4},{6,5},{7,6},{8,7},{9,8},{10,9},{11,1... | collective-permute-start | bytes 12296 | tf_op jit(solution)/shard_map/ppermute | solution.py:20
  15.6 0.1 fusion.83
  15.7 3.5 %collective-permute-done.3 = f32[4,1,256]{2,1,0:T(1,128)S(1)} collective-permute-done((f32[4,1,256]{2,1,0:T(1,128)S(1)}, f32[4,1,256]{2,1,0:T(1,128)S(1)}, u32[]{:S(2)}, u32[]{:S(2)}) %collective-permute-start.3) | collective-permute-done | bytes 4128 | tf_op jit(solution)/shard_map/ppermute | solution.py:20
  19.2 0.2 fusion.41
  19.5 0.1 copy.39
  19.7 0.1 copy.51
  19.8 2.4 %fusion.63 = f32[128,8,2,256]{3,1,2,0:T(8,128)} fusion(f32[2,256,128,1]{2,1,0,3:T(8,128)S(1)} %bitcast.131, s32[32,8]{1,0:T(8,128)S(1)} %multiply_add_fusion, s32[128]{0:T(128)S(1)} %multiply_add_fusion.1), kind=kOutput, calls=%fused_computation.81 | convolution fusion | flops 201359360 | bytes 2360832 | tf_op jit(solution)/shard_map/concatenate | solution.py:78
  22.2 17.7 %all-to-all-start = ((f32[128,8,2,256]{3,1,2,0:T(8,128)}), f32[128,8,2,256]{3,1,2,0:T(8,128)S(1)}, u32[]{:S(2)}, u32[]{:S(2)}) async-start(f32[128,8,2,256]{3,1,2,0:T(8,128)} %fusion.63), calls=%async_computation | async-start | bytes 4194304 | tf_op jit(solution)/shard_map/all_to_all | solution.py:81
  39.9 2.2 %copy.35 = s32[6144,2]{1,0:T(8,128)} copy(s32[6144,2]{0,1:T(2,128)S(1)} %compare_convert_fusion) | data formatting | bytes 98304 | tf_op jit(solution)/shard_map/convert_element_type | solution.py:84
  42.1 3.3 %reshape.209 = s32[96,128]{1,0:T(8,128)S(1)} reshape(s32[6144,2]{1,0:T(8,128)} %copy.35) | data formatting | bytes 98304 | tf_op jit(solution)/shard_map/convert_element_type | solution.py:84
  45.4 0.3 reduce_window_sum.22
  45.7 2.2 %copy.37 = s32[6144,2]{1,0:T(8,128)} copy(s32[6144,2]{0,1:T(2,128)S(1)} %copy-done.5) | data formatting | bytes 98304 | tf_op args[4]
  47.9 3.9 %mul.207 = s32[96,128]{1,0:T(8,128)} reshape(s32[6144,2]{1,0:T(8,128)} %copy.37) | data formatting | bytes 98304 | tf_op jit(solution)/shard_map/mul | solution.py:92
  51.8 2.2 %copy.36 = s32[6144,2]{1,0:T(8,128)} copy(s32[6144,2]{0,1:T(2,128)S(1)} %copy-done.6) | data formatting | bytes 98304 | tf_op args[3]
  54.0 4.0 %mul.204 = s32[96,128]{1,0:T(8,128)} reshape(s32[6144,2]{1,0:T(8,128)} %copy.36) | data formatting | bytes 98304 | tf_op jit(solution)/shard_map/mul | solution.py:88
  58.0 6.4 %select_reduce_fusion = (s32[96,8]{1,0:T(8,128)S(1)}, s32[96,8]{1,0:T(8,128)}, s32[96,8]{1,0:T(8,128)}) fusion(s32[96,128]{1,0:T(8,128)S(1)} %reshape.209, s32[96,128]{1,0:T(8,128)S(1)} %sub.47, s32[96,128]{1,0:T(8,128)} %mul.207, s32[96,128]{1,0:T(8,128)} %mul.204), kind=kLoop, calls=%fused_computation.35 | loop fusion | flops 685824 | bytes 205824 | tf_op jit(solution)/shard_map/reduce_sum | solution.py:94
  64.4 1.5 %eq.184 = s32[768]{0:T(1024)} reshape(s32[96,8]{1,0:T(8,128)} %get-tuple-element.4) | data formatting | bytes 6144 | tf_op jit(solution)/shard_map/eq | solution.py:103
  65.9 0.6 gt.16
  66.5 1.4 %compare_convert_fusion.4 = (f32[96,8]{1,0:T(8,128)S(1)}, f32[96,8]{1,0:T(8,128)}, f32[96,8]{1,0:T(8,128)S(1)}, f32[96,8]{1,0:T(8,128)S(1)}) fusion(s32[96,8]{1,0:T(8,128)} %get-tuple-element.3), kind=kLoop, calls=%fused_computation.112 | loop fusion | flops 6144 | bytes 15360 | tf_op jit(solution)/shard_map/convert_element_type | solution.py:100
  67.9 1.5 %reshape.213 = f32[768]{0:T(1024)} reshape(f32[96,8]{1,0:T(8,128)} %get-tuple-element.27) | data formatting | bytes 6144 | tf_op jit(solution)/shard_map/convert_element_type | solution.py:100
  69.4 0.7 reshape.212
  70.1 0.1 reshape.211
  70.2 0.1 reshape.210
  70.3 0.3 all-to-all-done
  70.5 1.6 %fusion.2 = f32[768,2,256]{0,2,1:T(8,128)S(1)} fusion(f32[4,256,256]{2,1,0:T(8,128)S(1)} %copy-done.1, f32[128,8,2,256]{3,1,2,0:T(8,128)S(1)} %all-to-all-done), kind=kOutput, calls=%fused_computation.2 | convolution fusion | flops 1207959552 | bytes 3407872 | tf_op jit(solution)/shard_map/sfc,cd->sfd/dot_general | solution.py:97
  72.1 1.6 %fusion.4 = f32[768,2,256]{0,2,1:T(8,128)S(1)} fusion(f32[4,256,256]{2,1,0:T(8,128)S(1)} %copy-done.1, f32[128,8,2,256]{3,1,2,0:T(8,128)S(1)} %all-to-all-done), kind=kOutput, calls=%fused_computation.4 | convolution fusion | flops 1207959552 | bytes 3407872 | tf_op jit(solution)/shard_map/sfc,cd->sfd/dot_general | solution.py:97
  73.7 1.6 %fusion.6 = f32[768,2,256]{0,2,1:T(8,128)S(1)} fusion(f32[4,256,256]{2,1,0:T(8,128)S(1)} %copy-done.1, f32[128,8,2,256]{3,1,2,0:T(8,128)S(1)} %all-to-all-done), kind=kOutput, calls=%fused_computation.6 | convolution fusion | flops 1207959552 | bytes 3407872 | tf_op jit(solution)/shard_map/sfc,cd->sfd/dot_general | solution.py:97
  75.3 1.6 %fusion.8 = f32[768,2,256]{0,2,1:T(8,128)S(1)} fusion(f32[4,256,256]{2,1,0:T(8,128)S(1)} %copy-done.1, f32[128,8,2,256]{3,1,2,0:T(8,128)S(1)} %all-to-all-done), kind=kOutput, calls=%fused_computation.8 | convolution fusion | flops 1207959552 | bytes 3407872 | tf_op jit(solution)/shard_map/sfc,cd->sfd/dot_general | solution.py:97
  76.9 1.3 %fusion = f32[64,2,256]{2,0,1:T(8,128)S(1)} fusion(f32[768,2,256]{0,2,1:T(8,128)S(1)} %fusion.2, f32[768,2,256]{0,2,1:T(8,128)S(1)} %fusion.4, f32[768,2,256]{0,2,1:T(8,128)S(1)} %fusion.6, f32[768,2,256]{0,2,1:T(8,128)S(1)} %fusion.8, f32[768]{0:T(1024)S(1)} %copy-done.8, f32[768]{0:T(1024)S(1)} %copy-done.9, f32[768]{0:T(1024)S(1)} %reshape.211, ...), kind=kOutput, calls=%fused_computation | convolution fusion | flops 304840704 | bytes 6438656 | tf_op jit(solution)/shard_map/dot_general | solution.py:106
  78.2 0.5 fusion.17
  78.8 1.0 concatenate.47
  79.8 9.5 %all-to-all-start.1 = ((f32[128,8,256]{2,1,0:T(8,128)}), f32[128,8,256]{2,1,0:T(8,128)S(1)}, u32[]{:S(2)}, u32[]{:S(2)}) async-start(f32[128,8,256]{2,1,0:T(8,128)} %concatenate.47), calls=%async_computation.1 | async-start | bytes 2097152 | tf_op jit(solution)/shard_map/all_to_all | solution.py:121
  89.3 0.8 compare_convert_fusion.5
  90.1 0.1 copy.46
  90.2 0.1 reshape.214
  90.3 0.1 copy.47
  90.4 0.1 reshape.215
  90.6 0.1 copy.48
  90.7 0.1 reshape.216
  90.8 0.1 copy.49
  90.9 0.1 reshape.217
  91.1 17.8 %all-to-all-done.1 = f32[128,8,256]{2,1,0:T(8,128)S(1)} async-done(((f32[128,8,256]{2,1,0:T(8,128)}), f32[128,8,256]{2,1,0:T(8,128)S(1)}, u32[]{:S(2)}, u32[]{:S(2)}) %all-to-all-start.1) | async-done | bytes 1048608 | tf_op jit(solution)/shard_map/all_to_all | solution.py:121
  108.9 0.3 fusion.31
  109.2 0.4 convolution_multiply_fusion.4
  109.6 0.4 fusion.24
  110.0 0.4 fusion.23
  110.4 0.4 fusion.22
  110.9 0.2 reduce_sum.49
  111.1 0.7 select_bitcast_fusion
  111.8 0.7 fusion.42
  (43 shorter events, 0.3 us)
Async XLA Ops:
  0.6 9.3 %copy-start = (f32[1,4,64,256]{3,2,1,0:T(8,128)S(1)}, f32[1,4,64,256]{3,2,1,0:T(8,128)}, u32[]{:S(2)}) copy-start(f32[1,4,64,256]{3,2,1,0:T(8,128)} %param.7) | copy-start | bytes 786436
  0.6 8.4 %copy-start.3 = (f32[1,2,64,256]{3,2,1,0:T(8,128)S(1)}, f32[1,2,64,256]{3,2,1,0:T(8,128)}, u32[]{:S(2)}) copy-start(f32[1,2,64,256]{3,2,1,0:T(8,128)} %param.8) | copy-start | bytes 393220
  0.7 8.4 %copy-start.4 = (s32[6144,2]{0,1:T(2,128)S(1)}, s32[6144,2]{0,1:T(2,128)}, u32[]{:S(2)}) copy-start(s32[6144,2]{0,1:T(2,128)} %param.9) | copy-start | bytes 147460
  1.5 8.4 %collective-permute-start = (f32[4,1,256]{2,1,0:T(1,128)S(1)}, f32[4,1,256]{2,1,0:T(1,128)S(1)}, u32[]{:S(2)}, u32[]{:S(2)}) collective-permute-start(f32[4,1,256]{2,1,0:T(1,128)S(1)} %get-tuple-element.15), channel_id=1, source_target_pairs={{0,1},{1,2},{2,3},{3,4},{4,5},{5,6},{6,7},{7,8},{8,9},{9,10},{10,1... | collective-permute-start | bytes 12296 | tf_op jit(solution)/shard_map/ppermute | solution.py:19
  5.5 4.4 %collective-permute-start.1 = (f32[4,1,256]{2,1,0:T(1,128)S(1)}, f32[4,1,256]{2,1,0:T(1,128)S(1)}, u32[]{:S(2)}, u32[]{:S(2)}) collective-permute-start(f32[4,1,256]{2,1,0:T(1,128)S(1)} %get-tuple-element.14), channel_id=1, source_target_pairs={{1,0},{2,1},{3,2},{4,3},{5,4},{6,5},{7,6},{8,7},{9,8},{10,9},{11,1... | collective-permute-start | bytes 12296 | tf_op jit(solution)/shard_map/ppermute | solution.py:20
  9.9 9.9 %copy-start.11 = (s32[128]{0:T(128)}, s32[128]{0:T(128)S(1)}, u32[]{:S(2)}) copy-start(s32[128]{0:T(128)S(1)} %multiply_add_fusion.1) | copy-start | bytes 1540
  10.3 5.4 %collective-permute-start.2 = (f32[4,1,256]{2,1,0:T(1,128)S(1)}, f32[4,1,256]{2,1,0:T(1,128)S(1)}, u32[]{:S(2)}, u32[]{:S(2)}) collective-permute-start(f32[4,1,256]{2,1,0:T(1,128)S(1)} %get-tuple-element.9), channel_id=1, source_target_pairs={{0,1},{1,2},{2,3},{3,4},{4,5},{5,6},{6,7},{7,8},{8,9},{9,10},{10,1... | collective-permute-start | bytes 12296 | tf_op jit(solution)/shard_map/ppermute | solution.py:19
  14.3 4.9 %collective-permute-start.3 = (f32[4,1,256]{2,1,0:T(1,128)S(1)}, f32[4,1,256]{2,1,0:T(1,128)S(1)}, u32[]{:S(2)}, u32[]{:S(2)}) collective-permute-start(f32[4,1,256]{2,1,0:T(1,128)S(1)} %get-tuple-element.8), channel_id=1, source_target_pairs={{1,0},{2,1},{3,2},{4,3},{5,4},{6,5},{7,6},{8,7},{9,8},{10,9},{11,1... | collective-permute-start | bytes 12296 | tf_op jit(solution)/shard_map/ppermute | solution.py:20
  22.2 48.4 %all-to-all-start = ((f32[128,8,2,256]{3,1,2,0:T(8,128)}), f32[128,8,2,256]{3,1,2,0:T(8,128)S(1)}, u32[]{:S(2)}, u32[]{:S(2)}) async-start(f32[128,8,2,256]{3,1,2,0:T(8,128)} %fusion.63), calls=%async_computation | async-start | bytes 4194304 | tf_op jit(solution)/shard_map/all_to_all | solution.py:81
  42.1 3.6 %copy-start.5 = (s32[6144,2]{0,1:T(2,128)S(1)}, s32[6144,2]{0,1:T(2,128)}, u32[]{:S(2)}) copy-start(s32[6144,2]{0,1:T(2,128)} %param.11) | copy-start | bytes 147460
  47.9 3.9 %copy-start.6 = (s32[6144,2]{0,1:T(2,128)S(1)}, s32[6144,2]{0,1:T(2,128)}, u32[]{:S(2)}) copy-start(s32[6144,2]{0,1:T(2,128)} %param.10) | copy-start | bytes 147460
  54.0 16.6 %copy-start.1 = (f32[4,256,256]{2,1,0:T(8,128)S(1)}, f32[4,256,256]{2,1,0:T(8,128)}, u32[]{:S(2)}) copy-start(f32[4,256,256]{2,1,0:T(8,128)} %param.12) | copy-start | bytes 3145732
  75.3 1.6 %copy-start.7 = (s32[768]{0:T(1024)S(1)}, s32[768]{0:T(1024)}, u32[]{:S(2)}) copy-start(s32[768]{0:T(1024)} %eq.184) | copy-start | bytes 9220
  75.3 1.6 %copy-start.8 = (f32[768]{0:T(1024)S(1)}, f32[768]{0:T(1024)}, u32[]{:S(2)}) copy-start(f32[768]{0:T(1024)} %reshape.213) | copy-start | bytes 9220
  75.3 1.6 %copy-start.9 = (f32[768]{0:T(1024)S(1)}, f32[768]{0:T(1024)}, u32[]{:S(2)}) copy-start(f32[768]{0:T(1024)} %reshape.212) | copy-start | bytes 9220
  75.3 1.6 %copy-start.10 = (pred[768]{0:T(1024)(128)(4,1)S(1)}, pred[768]{0:T(1024)(128)(4,1)}, u32[]{:S(2)}) copy-start(pred[768]{0:T(1024)(128)(4,1)} %gt.16) | copy-start | bytes 2308
  76.9 1.3 %copy-start.2 = (s32[64,256]{1,0:T(8,128)S(1)}, s32[64,256]{1,0:T(8,128)}, u32[]{:S(2)}) copy-start(s32[64,256]{1,0:T(8,128)} %param.13) | copy-start | bytes 196612
  79.8 29.1 %copy-start.12 = (s32[128]{0:T(128)S(1)}, s32[128]{0:T(128)}, u32[]{:S(2)}) copy-start(s32[128]{0:T(128)} %copy-done.11) | copy-start | bytes 1540
  79.8 29.1 %all-to-all-start.1 = ((f32[128,8,256]{2,1,0:T(8,128)}), f32[128,8,256]{2,1,0:T(8,128)S(1)}, u32[]{:S(2)}, u32[]{:S(2)}) async-start(f32[128,8,256]{2,1,0:T(8,128)} %concatenate.47), calls=%async_computation.1 | async-start | bytes 2097152 | tf_op jit(solution)/shard_map/all_to_all | solution.py:121
where the time goes:
time: 113 us; the launch traced here: 112 us
  starting transfers between devices  37.7 us (33%)
  local copies, waits for them, and re-layouts  28.2 us (25%)
  waiting for transfers between devices  21.6 us (19%)
  matrix products  12.4 us (11%)
  other arithmetic  11.4 us (10%)
  between operations  1.16 us (1%)
    all_to_all x1, waiting for transfers between devices, local(): lax.all_to_all(back_full, ('sec', 'tile'), split_axis=0, concat_axis=0, t...  17.8 us
    all_to_all x1, starting transfers between devices, local(): lax.all_to_all(outgoing, ('sec', 'tile'), split_axis=0, concat_axis=0, ti...  17.7 us
    all_to_all x1, starting transfers between devices, local(): lax.all_to_all(back_full, ('sec', 'tile'), split_axis=0, concat_axis=0, t...  9.49 us
    ppermute x2, starting transfers between devices, with_halo(): before = lax.ppermute(last, axis, up)  8 us
    reduce_sum x1, other arithmetic, local(): slot_valid = jnp.sum(slot_hot, axis=2).reshape(-1)  6.4 us
    dot_general x4, matrix products, local(): jnp.einsum('sfc,cd->sfd', from_atmos, tables[table_ordinal], precision=la...  6.26 us
    convert_element_type x2, local copies, waits for them, and re-layouts, local(): mine = (all_owner == tile_index).astype(jnp.int32)  5.49 us
    unnamed x29, local copies, waits for them, and re-layouts  4.47 us
  transfers between devices with their start and end apart: 6, of which 3 were waited for; matrix products, arithmetic and copies ran while one was open for 31% of the time, Pallas kernels for 0%

commit v1 on v0

v1 whole, which is shorter than its diff:
```python
import functools

import jax
import jax.numpy as jnp
from jax import lax
from jax.experimental import pallas as pl
from jax.experimental.pallas import tpu as pltpu
from jax.sharding import PartitionSpec as P

forcing_rate = 0.5

F32 = jnp.float32
BF16 = jnp.bfloat16
PAD = 8


def matmul(a, b):
    return lax.dot_general(a, b, (((1,), (0,)), ((), ())), preferred_element_type=F32)


def split(x):
    hi = x.astype(BF16)
    return hi, (x - hi.astype(F32)).astype(BF16)


def iota(shape, dim):
    return lax.broadcasted_iota(jnp.int32, shape, dim)


def kernel(
    n_sec, n_tile, cap,
    fields, coef, ot_in, db_in, ti_in, tables, mask_in,
    fo, su,
    ext, cext, mid, ot, db, ti, tab, mask, hsend, hrecv,
    thi, tlo, tthi, ttlo, mmat, mtmat, pthi, ptlo, send, recv,
    x0, x1, d0, d1, smat, rmat, ret, arr,
    in_sem, hs_sem, hr_sem, fs_sem, fr_sem, bs_sem, br_sem,
):
    n_atm = n_sec - 1
    ocean_sec = n_sec - 1
    half = n_tile // 2
    levels, rows, width = fo.shape[1:]
    ntab = tables.shape[0]
    top, low = PAD, PAD + rows
    sec = lax.axis_index("sec")
    tile = lax.axis_index("tile")
    upper = lax.rem(tile + n_tile - 1, n_tile)
    lower = lax.rem(tile + 1, n_tile)
    is_ocean = sec == ocean_sec
    parity = lax.rem(tile, 2)

    def load(number, src, dst):
        return pltpu.make_async_copy(src, dst, in_sem.at[number])

    loads = [
        load(0, fields.at[0], ext.at[:, top:low, :]),
        load(1, coef.at[0], cext.at[:, top:low, :]),
        load(2, ot_in, ot),
        load(3, db_in, db),
        load(4, ti_in, ti),
        load(5, tables, tab),
        load(6, mask_in, mask),
    ]
    for copy in loads:
        copy.start()

    barrier = pltpu.get_barrier_semaphore()

    def greet(s, t):
        pl.semaphore_signal(barrier, inc=1, device_id=(s, t), device_id_type=pl.DeviceIdType.MESH)

    greet(sec, upper)
    greet(sec, lower)

    @pl.when(is_ocean)
    def _():
        for a in range(n_atm):
            lax.fori_loop(0, n_tile, lambda k, c: (greet(a, lax.rem(tile + k, n_tile)), c)[1], 0)

    @pl.when(jnp.logical_not(is_ocean))
    def _():
        lax.fori_loop(0, n_tile, lambda k, c: (greet(ocean_sec, lax.rem(tile + k, n_tile)), c)[1], 0)

    zero = jnp.zeros((PAD, width), F32)
    for l in range(levels):
        ext[l, 0:top, :] = zero
        ext[l, low : low + PAD, :] = zero
    for c in range(2):
        cext[c, 0:top, :] = zero
        cext[c, low : low + PAD, :] = zero
        hsend[c, 8:16, :] = zero
    loads[0].wait()
    for l in range(levels):
        hsend[0, 2 * l : 2 * l + 2, :] = ext[l, top : top + 2, :]
        hsend[1, 2 * l : 2 * l + 2, :] = ext[l, low - 2 : low, :]
    loads[1].wait()
    for c in range(2):
        hsend[0, 8 + c : 9 + c, :] = cext[c, top : top + 1, :]
        hsend[1, 8 + c : 9 + c, :] = cext[c, low - 1 : low, :]

    @pl.when(is_ocean)
    def _():
        pl.semaphore_wait(barrier, 2 + n_atm * n_tile)

    @pl.when(jnp.logical_not(is_ocean))
    def _():
        pl.semaphore_wait(barrier, 2 + n_tile)

    def halo(way, to):
        return pltpu.make_async_remote_copy(
            src_ref=hsend.at[way],
            dst_ref=hrecv.at[1 - way],
            send_sem=hs_sem.at[way],
            recv_sem=hr_sem.at[1 - way],
            device_id=(sec, to),
            device_id_type=pl.DeviceIdType.MESH,
        )

    halos = [halo(0, upper), halo(1, lower)]
    for copy in halos:
        copy.start()

    loads[2].wait()
    loads[3].wait()
    loads[4].wait()
    loads[5].wait()
    loads[6].wait()

    lane = iota((8, 128), 1)
    left = lane < 64

    @pl.when(is_ocean)
    def _():
        mine_of = tile.astype(F32)
        pair_rows = x0.shape[0]
        for k in range(pair_rows):
            cols = slice(128 * k, 128 * (k + 1))
            x0[k : k + 1, :] = ot[0:1, cols].astype(F32)
            x1[k : k + 1, :] = ot[1:2, cols].astype(F32)
            d0[k : k + 1, :] = db[0:1, cols].astype(F32) + 1.0
            d1[k : k + 1, :] = db[1:2, cols].astype(F32) + 1.0
        src, dst = iota((128, 128), 0), iota((128, 128), 1)
        same = (src // 64) == (dst // 64)
        both = same.astype(F32).astype(BF16)
        before = (same & (src < dst)).astype(F32).astype(BF16)
        mine0 = x0[...] == mine_of
        mine1 = x1[...] == mine_of
        m0 = mine0.astype(F32).astype(BF16)
        m1 = mine1.astype(F32).astype(BF16)
        x0[...] = jnp.where(mine0, matmul(m0, before), -1.0)
        x1[...] = jnp.where(mine1, matmul(m1, before) + matmul(m0, both), -1.0)
        slot = iota((cap, 128), 0).astype(F32)
        lane_c = iota((half * cap, 128), 1)
        want = (lax.rem(lane_c, 64) + 1).astype(F32)
        left_c = lane_c < 64
        for a in range(n_atm):
            parts = []
            for kk in range(half):
                k = a * half + kk
                parts.append(
                    jnp.where(x0[k : k + 1, :] == slot, d0[k : k + 1, :], 0.0)
                    + jnp.where(x1[k : k + 1, :] == slot, d1[k : k + 1, :], 0.0)
                )
            named = jnp.concatenate(parts, axis=0).astype(BF16)
            hot = (matmul(named, both) == want).astype(F32)
            turned = hot.T
            count = half * cap
            smat[a, :, 0:count] = turned[0:64].astype(BF16)
            smat[a, :, count : 2 * count] = turned[64:128].astype(BF16)
            other = pltpu.roll(hot, 64, 1)
            rmat[a, 0:count, :] = jnp.where(left_c, hot, other).astype(BF16)
            rmat[a, count : 2 * count, :] = jnp.where(left_c, other, hot).astype(BF16)

    @pl.when(jnp.logical_not(is_ocean))
    def _():
        number = sec * n_tile + tile
        cols = pl.ds(pl.multiple_of((number // 2) * 128, 128), 128)

        def pairs(ref):
            r0 = jnp.broadcast_to(ref[0:1, cols].astype(F32), (8, 128))
            r1 = jnp.broadcast_to(ref[1:2, cols].astype(F32), (8, 128))
            even = jnp.where(left, r0, pltpu.roll(r1, 64, 1))
            odd = jnp.where(left, pltpu.roll(r0, 64, 1), r1)
            return jnp.where(parity == 0, even, odd)

        own, entry = pairs(ot), pairs(ti)
        across = jnp.broadcast_to(own[0:1], (128, 128))
        earlier = (across.T == across) & (iota((128, 128), 0) < iota((128, 128), 1))
        rank = jnp.sum(earlier.astype(F32), axis=0, keepdims=True)
        target = own * float(cap) + jnp.broadcast_to(rank, (8, 128))

        def doubled(v):
            turned = pltpu.roll(v, 64, 1)
            return jnp.where(left, v, turned), jnp.where(left, turned, v)

        t0, t1 = doubled(target)
        e0, e1 = doubled(entry)
        slots = iota((n_tile * cap, 128), 0).astype(F32)
        for b in range(ntab // 2):
            here = (lane // 64 + 2 * b).astype(F32)
            v0 = jnp.where(e0 == here, t0, -1.0)
            v1 = jnp.where(e1 == here, t1, -1.0)
            hot = ((slots == v0[0:1]) | (slots == v1[0:1])).astype(F32)
            mmat[:, 128 * b : 128 * (b + 1)] = hot.astype(BF16)
            mtmat[128 * b : 128 * (b + 1), :] = hot.T.astype(BF16)
        for t in range(ntab):
            hi, lo = split(tab[t])
            thi[t] = hi
            tlo[t] = lo

    for copy in halos:
        copy.wait()
    above = jnp.where(tile > 0, hrecv[0], 0.0)
    below = jnp.where(tile < n_tile - 1, hrecv[1], 0.0)
    for l in range(levels):
        ext[l, top - 2 : top, :] = above[2 * l : 2 * l + 2]
        ext[l, low : low + 2, :] = below[2 * l : 2 * l + 2]
    for c in range(2):
        cext[c, top - 1 : top, :] = above[8 + c : 9 + c]
        cext[c, low : low + 1, :] = below[8 + c : 9 + c]

    def substep(u, kappa, speed):
        n = u.shape[0]
        up = pltpu.roll(u, 1, 0)
        down = pltpu.roll(u, n - 1, 0)
        sides = pltpu.roll(u, 1, 1) + pltpu.roll(u, width - 1, 1)
        return u + kappa * (up + down + sides - 4.0 * u) - 0.5 * speed * (down - up)

    def stencil(l):
        kappa, speed = cext[0], cext[1]
        u = substep(ext[l], kappa, speed)
        return substep(u, kappa, speed)[top:low]

    fo[0, 0] = stencil(0)
    fo[0, 1] = stencil(1)

    @pl.when(jnp.logical_not(is_ocean))
    def _():
        f0, f1 = fo[0, 0], fo[0, 1]
        phi, plo = split(jnp.concatenate([f0, f0 - f1], axis=0))
        pall = jnp.concatenate([phi, plo], axis=0)
        for t in range(ntab):
            r = matmul(pall, thi[t])
            r = r[: 2 * rows] + r[2 * rows :] + matmul(phi, tlo[t])
            for c in range(2):
                hi, lo = split(r[c * rows : (c + 1) * rows])
                pthi[t * rows : (t + 1) * rows, c * width : (c + 1) * width] = hi
                ptlo[t * rows : (t + 1) * rows, c * width : (c + 1) * width] = lo
        out = matmul(mmat[...], pthi[...]) + matmul(mmat[...], ptlo[...])
        send[...] = out.reshape(send.shape)

        def ship(k, c):
            o = lax.rem(tile + k, n_tile)
            pltpu.make_async_remote_copy(
                src_ref=send.at[o],
                dst_ref=recv.at[sec, parity, tile // 2],
                send_sem=fs_sem,
                recv_sem=fr_sem.at[sec],
                device_id=(ocean_sec, o),
                device_id_type=pl.DeviceIdType.MESH,
            ).start()
            return c

        lax.fori_loop(0, n_tile, ship, 0)
        for l in range(2, levels):
            fo[0, l] = stencil(l)
        for t in range(ntab):
            hi, lo = split(tab[t].T)
            tthi[t] = hi
            ttlo[t] = lo
        pltpu.make_async_copy(arr, arr, br_sem).wait()
        uhi, ulo = split(arr[...].reshape(n_tile * cap, width))
        v = matmul(mtmat[...], uhi) + matmul(mtmat[...], ulo)
        total = jnp.zeros((rows, width), F32)
        for t in range(ntab):
            vhi, vlo = split(v[t * rows : (t + 1) * rows])
            r = matmul(jnp.concatenate([vhi, vlo], axis=0), tthi[t])
            total = total + r[:rows] + r[rows:] + matmul(vhi, ttlo[t])
        su[0] = total
        pltpu.make_async_copy(send, send, fs_sem).wait()

    @pl.when(is_ocean)
    def _():
        for l in range(2, levels):
            fo[0, l] = stencil(l)
        flux = jnp.zeros((rows, 2 * width), F32)
        for a in range(n_atm):
            pltpu.make_async_copy(recv.at[a], recv.at[a], fr_sem.at[a]).wait()
            hi, lo = split(recv[a].reshape(n_tile * cap, 2 * width))
            flux = flux + matmul(smat[a], hi) + matmul(smat[a], lo)
        water = mask[...].astype(F32)
        first = fo[0, 0] + forcing_rate * water * flux[:, :width]
        second = fo[0, 1] + forcing_rate * water * flux[:, width:]
        sea = water * first
        hi, lo = split(sea)
        both = jnp.concatenate([hi, lo], axis=0)
        for a in range(n_atm):
            ret[a] = matmul(rmat[a], both).reshape(ret.shape[1:])

            def back(k, c):
                t = lax.rem(tile + k, n_tile)
                pltpu.make_async_remote_copy(
                    src_ref=ret.at[a, lax.rem(t, 2), t // 2],
                    dst_ref=arr.at[tile],
                    send_sem=bs_sem,
                    recv_sem=br_sem,
                    device_id=(a, t),
                    device_id_type=pl.DeviceIdType.MESH,
                ).start()
                return c

            lax.fori_loop(0, n_tile, back, 0)
        fo[0, 0] = first
        fo[0, 1] = second
        su[0] = sea
        pltpu.make_async_copy(ret, ret, bs_sem).wait()


def local(fields, coefficients, owner_tile, dest_block, table_index, tables, land_mask):
    n_sec = lax.axis_size("sec")
    n_tile = lax.axis_size("tile")
    _, levels, rows, width = fields.shape
    blocks, fan_out = owner_tile.shape
    ntab = tables.shape[0]
    cap = 2 * fan_out * rows // n_tile
    n_atm = n_sec - 1
    half = n_tile // 2
    padded = rows + 2 * PAD
    slots = n_tile * cap
    scratch = [
        pltpu.VMEM((levels, padded, width), F32),
        pltpu.VMEM((2, padded, width), F32),
        pltpu.VMEM((levels, padded, width), F32),
        pltpu.VMEM((fan_out, blocks), jnp.int32),
        pltpu.VMEM((fan_out, blocks), jnp.int32),
        pltpu.VMEM((fan_out, blocks), jnp.int32),
        pltpu.VMEM((ntab, width, width), F32),
        pltpu.VMEM((rows, width), jnp.int32),
        pltpu.VMEM((2, 16, width), F32),
        pltpu.VMEM((2, 16, width), F32),
        pltpu.VMEM((ntab, width, width), BF16),
        pltpu.VMEM((ntab, width, width), BF16),
        pltpu.VMEM((ntab, width, width), BF16),
        pltpu.VMEM((ntab, width, width), BF16),
        pltpu.VMEM((slots, ntab * rows), BF16),
        pltpu.VMEM((ntab * rows, slots), BF16),
        pltpu.VMEM((ntab * rows, 2 * width), BF16),
        pltpu.VMEM((ntab * rows, 2 * width), BF16),
        pltpu.VMEM((n_tile, cap, 2 * width), F32),
        pltpu.VMEM((n_atm, 2, half, cap, 2 * width), F32),
        pltpu.VMEM((n_atm * half, 2 * rows), F32),
        pltpu.VMEM((n_atm * half, 2 * rows), F32),
        pltpu.VMEM((n_atm * half, 2 * rows), F32),
        pltpu.VMEM((n_atm * half, 2 * rows), F32),
        pltpu.VMEM((n_atm, rows, slots), BF16),
        pltpu.VMEM((n_atm, slots, 2 * rows), BF16),
        pltpu.VMEM((n_atm, 2, half, cap, width), F32),
        pltpu.VMEM((n_tile, cap, width), F32),
        pltpu.SemaphoreType.DMA((7,)),
        pltpu.SemaphoreType.DMA((2,)),
        pltpu.SemaphoreType.DMA((2,)),
        pltpu.SemaphoreType.DMA,
        pltpu.SemaphoreType.DMA((n_atm,)),
        pltpu.SemaphoreType.DMA,
        pltpu.SemaphoreType.DMA,
    ]
    return pl.pallas_call(
        functools.partial(kernel, n_sec, n_tile, cap),
        out_shape=(
            jax.ShapeDtypeStruct(fields.shape, F32),
            jax.ShapeDtypeStruct((1, rows, width), F32),
        ),
        in_specs=[pl.BlockSpec(memory_space=pl.ANY)] * 7,
        out_specs=(
            pl.BlockSpec(memory_space=pltpu.VMEM),
            pl.BlockSpec(memory_space=pltpu.VMEM),
        ),
        scratch_shapes=scratch,
        compiler_params=pltpu.CompilerParams(
            collective_id=0, has_side_effects=True, vmem_limit_bytes=32 * 1024 * 1024
        ),
    )(fields, coefficients, owner_tile.T, dest_block.T, table_index.T, tables, land_mask)


def solution(mesh):
    placed = (
        P("sec", None, "tile", None),
        P("sec", None, "tile", None),
        P(),
        P(),
        P(),
        P(),
        P("tile", None),
    )
    return jax.shard_map(
        local,
        mesh=mesh,
        in_specs=placed,
        out_specs=(P("sec", None, "tile", None), P("sec", "tile", None)),
        check_vma=False,
    )
```

time: 113 us -> 48.1 us (0.43)
  Pallas kernels: 0 us -> 39.4 us
  starting transfers between devices: 37.7 us -> 0 us
  waiting for transfers between devices: 21.6 us -> 0 us
  local copies, waits for them, and re-layouts: 28.2 us -> 7.64 us
  matrix products: 12.4 us -> 0 us
  other arithmetic: 11.4 us -> 0 us
    pallas_call x0 -> x1, Pallas kernels: none -> 39.4 us  [local(): pl.pallas_call(functools.partial(kernel, n_sec, n_tile, cap), out_shape=(...]
    all_to_all x2 -> x0, starting transfers between devices: 27.2 us -> none  [the longest x1 17.7 us: local(): lax.all_to_all(outgoing, ('sec', 'tile'), split_axis=0, concat_axis=0, ti...]
    all_to_all x2 -> x0, waiting for transfers between devices: 18.1 us -> none  [the longest x1 17.8 us: local(): lax.all_to_all(back_full, ('sec', 'tile'), split_axis=0, concat_axis=0, t...]
    ppermute x4 -> x0, starting transfers between devices: 10.6 us -> none  [the longest x2 8 us: with_halo(): before = lax.ppermute(last, axis, up)]
    dot_general x11 -> x0, matrix products: 10 us -> none  [the longest x4 6.26 us: local(): jnp.einsum('sfc,cd->sfd', from_atmos, tables[table_ordinal], precision=la...]
    convert_element_type x14 -> x0, local copies, waits for them, and re-layouts: 8.75 us -> none  [the longest x2 5.49 us: local(): mine = (all_owner == tile_index).astype(jnp.int32)]
    mul x3 -> x0, local copies, waits for them, and re-layouts: 7.98 us -> none  [the longest x1 3.97 us: local(): slot_hot * dest_block.reshape(atm_count, 1, pairs_count)]
    reduce_sum x3 -> x0, other arithmetic: 6.72 us -> none  [the longest x1 6.4 us: local(): slot_valid = jnp.sum(slot_hot, axis=2).reshape(-1)]
  transfers between devices with their start and end apart: 6 -> 0, of which waited for: 3 -> 0; matrix products, arithmetic and copies ran while one was open for 31% -> 0% of each run, Pallas kernels for 0% -> 0%
where the time goes in v1:
time: 48.1 us; the launch traced here: 47.7 us
  Pallas kernels  39.4 us (82%)
  local copies, waits for them, and re-layouts  7.64 us (16%)
  between operations  0.66 us (1%)
    pallas_call x1, Pallas kernels, local(): pl.pallas_call(functools.partial(kernel, n_sec, n_tile, cap), out_shape=(...  39.4 us
    unnamed x16, local copies, waits for them, and re-layouts  7.64 us

profile of v1, /device:TPU:1, one launch (start us, length us, event | category | flops | bytes accessed | tf_op | source)
XLA Modules:
  0.0 47.7 jit_solution(4377088259470777549)
XLA Ops:
  0.6 0.0 copy-start
  0.6 1.2 %copy-done = f32[4,256,256]{2,1,0:T(8,128)S(1)} copy-done((f32[4,256,256]{2,1,0:T(8,128)S(1)}, f32[4,256,256]{2,1,0:T(8,128)}, u32[]{:S(2)}) %copy-start) | copy-done | bytes 1048600
  1.9 0.0 copy-start.1
  1.9 0.9 %copy-done.1 = f32[1,4,64,256]{3,2,1,0:T(8,128)S(1)} copy-done((f32[1,4,64,256]{3,2,1,0:T(8,128)S(1)}, f32[1,4,64,256]{3,2,1,0:T(8,128)}, u32[]{:S(2)}) %copy-start.1) | copy-done | bytes 262168
  2.8 0.0 copy-start.2
  2.8 0.9 %copy-done.2 = f32[1,2,64,256]{3,2,1,0:T(8,128)S(1)} copy-done((f32[1,2,64,256]{3,2,1,0:T(8,128)S(1)}, f32[1,2,64,256]{3,2,1,0:T(8,128)}, u32[]{:S(2)}) %copy-start.2) | copy-done | bytes 131096
  3.7 0.0 copy-start.3
  3.7 0.8 %copy-done.3 = s32[64,256]{1,0:T(8,128)S(1)} copy-done((s32[64,256]{1,0:T(8,128)S(1)}, s32[64,256]{1,0:T(8,128)}, u32[]{:S(2)}) %copy-start.3) | copy-done | bytes 65560
  4.6 0.0 copy-start.4
  4.6 0.8 %copy-done.4 = s32[6144,2]{0,1:T(2,128)S(1)} copy-done((s32[6144,2]{0,1:T(2,128)S(1)}, s32[6144,2]{0,1:T(2,128)}, u32[]{:S(2)}) %copy-start.4) | copy-done | bytes 49176
  5.4 0.0 copy-start.5
  5.4 0.8 %copy-done.5 = s32[6144,2]{0,1:T(2,128)S(1)} copy-done((s32[6144,2]{0,1:T(2,128)S(1)}, s32[6144,2]{0,1:T(2,128)}, u32[]{:S(2)}) %copy-start.5) | copy-done | bytes 49176
  6.2 0.0 copy-start.6
  6.2 0.8 %copy-done.6 = s32[6144,2]{0,1:T(2,128)S(1)} copy-done((s32[6144,2]{0,1:T(2,128)S(1)}, s32[6144,2]{0,1:T(2,128)}, u32[]{:S(2)}) %copy-start.6) | copy-done | bytes 49176
  7.0 39.4 %shard_map.86 = (f32[1,4,64,256]{3,2,1,0:T(8,128)S(1)}, f32[1,64,256]{2,1,0:T(8,128)S(1)}) custom-call(f32[1,4,64,256]{3,2,1,0:T(8,128)S(1)} %copy-done.1, f32[1,2,64,256]{3,2,1,0:T(8,128)S(1)} %copy-done.2, s32[2,6144]{1,0:T(2,128)S(1)} %bitcast.3, s32[2,6144]{1,0:T(2,128)S(1)} %bitcast.4, s32[2,6144]{1,0:T(2,128)S(1)} %bitcast.5, ...), custom_call_target="tpu_custom_call" | custom-call | tf_op jit(solution)/shard_map/pallas_call | solution.py:367
  46.3 0.7 %copy.11 = f32[1,4,64,256]{3,2,1,0:T(8,128)} copy(f32[1,4,64,256]{3,2,1,0:T(8,128)S(1)} %get-tuple-element.4) | data formatting | bytes 524288
  47.0 0.6 %copy.12 = f32[1,64,256]{2,1,0:T(8,128)} copy(f32[1,64,256]{2,1,0:T(8,128)S(1)} %get-tuple-element.5) | data formatting | bytes 131072
Async XLA Ops:
  0.6 1.2 %copy-start = (f32[4,256,256]{2,1,0:T(8,128)S(1)}, f32[4,256,256]{2,1,0:T(8,128)}, u32[]{:S(2)}) copy-start(f32[4,256,256]{2,1,0:T(8,128)} %tables.1) | copy-start | bytes 3145732
  1.9 0.9 %copy-start.1 = (f32[1,4,64,256]{3,2,1,0:T(8,128)S(1)}, f32[1,4,64,256]{3,2,1,0:T(8,128)}, u32[]{:S(2)}) copy-start(f32[1,4,64,256]{3,2,1,0:T(8,128)} %fields.1) | copy-start | bytes 786436
  2.8 0.9 %copy-start.2 = (f32[1,2,64,256]{3,2,1,0:T(8,128)S(1)}, f32[1,2,64,256]{3,2,1,0:T(8,128)}, u32[]{:S(2)}) copy-start(f32[1,2,64,256]{3,2,1,0:T(8,128)} %coef.1) | copy-start | bytes 393220
  3.7 0.8 %copy-start.3 = (s32[64,256]{1,0:T(8,128)S(1)}, s32[64,256]{1,0:T(8,128)}, u32[]{:S(2)}) copy-start(s32[64,256]{1,0:T(8,128)} %mask_in.1) | copy-start | bytes 196612
  4.6 0.8 %copy-start.4 = (s32[6144,2]{0,1:T(2,128)S(1)}, s32[6144,2]{0,1:T(2,128)}, u32[]{:S(2)}) copy-start(s32[6144,2]{0,1:T(2,128)} %param.9) | copy-start | bytes 147460
  5.4 0.8 %copy-start.5 = (s32[6144,2]{0,1:T(2,128)S(1)}, s32[6144,2]{0,1:T(2,128)}, u32[]{:S(2)}) copy-start(s32[6144,2]{0,1:T(2,128)} %param.10) | copy-start | bytes 147460
  6.2 0.8 %copy-start.6 = (s32[6144,2]{0,1:T(2,128)S(1)}, s32[6144,2]{0,1:T(2,128)}, u32[]{:S(2)}) copy-start(s32[6144,2]{0,1:T(2,128)} %param.11) | copy-start | bytes 147460

commit v2 on v1

--- a/solution.py
+++ b/solution.py
@@ -31,13 +31,14 @@
     n_sec, n_tile, cap,
     fields, coef, ot_in, db_in, ti_in, tables, mask_in,
     fo, su,
-    ext, cext, mid, ot, db, ti, tab, mask, hsend, hrecv,
+    ext, cext, ot, db, ti, tab, mask, hsend, hrecv,
     thi, tlo, tthi, ttlo, mmat, mtmat, pthi, ptlo, send, recv,
-    x0, x1, d0, d1, smat, rmat, ret, arr,
-    in_sem, hs_sem, hr_sem, fs_sem, fr_sem, bs_sem, br_sem,
+    x0, x1, d0, d1, smat, rmat, ret, arr, mine_sum, far_sum,
+    in_sem, hs_sem, hr_sem, fs_sem, fr_sem, bs_sem, br_sem, ps_sem, pr_sem,
 ):
     n_atm = n_sec - 1
     ocean_sec = n_sec - 1
+    near_sec = n_sec - 2
     half = n_tile // 2
     levels, rows, width = fo.shape[1:]
     ntab = tables.shape[0]
@@ -47,7 +48,13 @@
     upper = lax.rem(tile + n_tile - 1, n_tile)
     lower = lax.rem(tile + 1, n_tile)
     is_ocean = sec == ocean_sec
+    is_near = sec == near_sec
+    is_far = sec < near_sec
     parity = lax.rem(tile, 2)
+
+    def flipped(t):
+        return t + 1 - 2 * lax.rem(t, 2)
+
 
     def load(number, src, dst):
         return pltpu.make_async_copy(src, dst, in_sem.at[number])
@@ -69,17 +76,32 @@
     def greet(s, t):
         pl.semaphore_signal(barrier, inc=1, device_id=(s, t), device_id_type=pl.DeviceIdType.MESH)
 
-    greet(sec, upper)
-    greet(sec, lower)
+    def greet_tiles(s, first):
+        def one(k, c):
+            greet(s, lax.rem(tile + k, n_tile))
+            return c
+
+        lax.fori_loop(first, n_tile, one, 0)
 
     @pl.when(is_ocean)
     def _():
         for a in range(n_atm):
-            lax.fori_loop(0, n_tile, lambda k, c: (greet(a, lax.rem(tile + k, n_tile)), c)[1], 0)
+            greet_tiles(a, 0)
+        greet(sec, upper)
+        greet(sec, lower)
 
     @pl.when(jnp.logical_not(is_ocean))
     def _():
-        lax.fori_loop(0, n_tile, lambda k, c: (greet(ocean_sec, lax.rem(tile + k, n_tile)), c)[1], 0)
+        greet_tiles(ocean_sec, 0)
+
+    @pl.when(is_far)
+    def _():
+        greet_tiles(sec, 1)
+
+    @pl.when(is_near)
+    def _():
+        greet(sec, upper)
+        greet(sec, lower)
 
     zero = jnp.zeros((PAD, width), F32)
     for l in range(levels):
@@ -102,7 +124,11 @@
     def _():
         pl.semaphore_wait(barrier, 2 + n_atm * n_tile)
 
-    @pl.when(jnp.logical_not(is_ocean))
+    @pl.when(is_far)
+    def _():
+        pl.semaphore_wait(barrier, n_tile - 1 + n_tile)
+
+    @pl.when(is_near)
     def _():
         pl.semaphore_wait(barrier, 2 + n_tile)
 
@@ -129,20 +155,18 @@
     lane = iota((8, 128), 1)
     left = lane < 64
 
-    @pl.when(is_ocean)
-    def _():
-        mine_of = tile.astype(F32)
-        pair_rows = x0.shape[0]
-        for k in range(pair_rows):
-            cols = slice(128 * k, 128 * (k + 1))
-            x0[k : k + 1, :] = ot[0:1, cols].astype(F32)
-            x1[k : k + 1, :] = ot[1:2, cols].astype(F32)
-            d0[k : k + 1, :] = db[0:1, cols].astype(F32) + 1.0
-            d1[k : k + 1, :] = db[1:2, cols].astype(F32) + 1.0
+    def place(number, a, owner):
+        for kk in range(half):
+            cols = pl.ds(pl.multiple_of((a * half + kk) * 128, 128), 128)
+            x0[kk : kk + 1, :] = ot[0:1, cols].astype(F32)
+            x1[kk : kk + 1, :] = ot[1:2, cols].astype(F32)
+            d0[kk : kk + 1, :] = db[0:1, cols].astype(F32) + 1.0
+            d1[kk : kk + 1, :] = db[1:2, cols].astype(F32) + 1.0
         src, dst = iota((128, 128), 0), iota((128, 128), 1)
         same = (src // 64) == (dst // 64)
         both = same.astype(F32).astype(BF16)
         before = (same & (src < dst)).astype(F32).astype(BF16)
+        mine_of = owner.astype(F32)
         mine0 = x0[...] == mine_of
         mine1 = x1[...] == mine_of
         m0 = mine0.astype(F32).astype(BF16)
@@ -150,26 +174,33 @@
         x0[...] = jnp.where(mine0, matmul(m0, before), -1.0)
         x1[...] = jnp.where(mine1, matmul(m1, before) + matmul(m0, both), -1.0)
         slot = iota((cap, 128), 0).astype(F32)
-        lane_c = iota((half * cap, 128), 1)
+        parts = []
+        for kk in range(half):
+            parts.append(
+                jnp.where(x0[kk : kk + 1, :] == slot, d0[kk : kk + 1, :], 0.0)
+                + jnp.where(x1[kk : kk + 1, :] == slot, d1[kk : kk + 1, :], 0.0)
+            )
+        named = jnp.concatenate(parts, axis=0).astype(BF16)
+        count = half * cap
+        lane_c = iota((count, 128), 1)
+        left_c = lane_c < 64
         want = (lax.rem(lane_c, 64) + 1).astype(F32)
-        left_c = lane_c < 64
+        hot = (matmul(named, both) == want).astype(F32)
+        turned = hot.T
+        smat[number, :, 0:count] = turned[0:64].astype(BF16)
+        smat[number, :, count : 2 * count] = turned[64:128].astype(BF16)
+        other = pltpu.roll(hot, 64, 1)
+        rmat[number, 0:count, :] = jnp.where(left_c, hot, other).astype(BF16)
+        rmat[number, count : 2 * count, :] = jnp.where(left_c, other, hot).astype(BF16)
+
+    @pl.when(is_ocean)
+    def _():
         for a in range(n_atm):
-            parts = []
-            for kk in range(half):
-                k = a * half + kk
-                parts.append(
-                    jnp.where(x0[k : k + 1, :] == slot, d0[k : k + 1, :], 0.0)
-                    + jnp.where(x1[k : k + 1, :] == slot, d1[k : k + 1, :], 0.0)
-                )
-            named = jnp.concatenate(parts, axis=0).astype(BF16)
-            hot = (matmul(named, both) == want).astype(F32)
-            turned = hot.T
-            count = half * cap
-            smat[a, :, 0:count] = turned[0:64].astype(BF16)
-            smat[a, :, count : 2 * count] = turned[64:128].astype(BF16)
-            other = pltpu.roll(hot, 64, 1)
-            rmat[a, 0:count, :] = jnp.where(left_c, hot, other).astype(BF16)
-            rmat[a, count : 2 * count, :] = jnp.where(left_c, other, hot).astype(BF16)
+            place(a, a, tile)
+
+    @pl.when(is_far)
+    def _():
+        place(0, sec, flipped(tile))
 
     @pl.when(jnp.logical_not(is_ocean))
     def _():
@@ -232,42 +263,92 @@
         return substep(u, kappa, speed)[top:low]
 
     fo[0, 0] = stencil(0)
-    fo[0, 1] = stencil(1)
+
+    def pack(part, row):
+        hi, lo = split(row)
+        stacked = jnp.concatenate([hi, lo], axis=0)
+        for t in range(ntab):
+            r = matmul(stacked, thi[t])
+            r = r[:rows] + r[rows:] + matmul(hi, tlo[t])
+            here = slice(t * rows, (t + 1) * rows)
+            pthi[here, :], ptlo[here, :] = split(r)
+        out = matmul(mmat[...], pthi[...]) + matmul(mmat[...], ptlo[...])
+        send[part] = out.reshape(send.shape[1:])
+
+    def ship(part, o, to):
+        pltpu.make_async_remote_copy(
+            src_ref=send.at[part, o],
+            dst_ref=recv.at[part, sec, parity, tile // 2],
+            send_sem=fs_sem.at[part],
+            recv_sem=fr_sem.at[part, sec],
+            device_id=to,
+            device_id_type=pl.DeviceIdType.MESH,
+        ).start()
+
+    def ship_to_ocean(part):
+        def one(k, c):
+            o = lax.rem(tile + k, n_tile)
+            ship(part, o, (ocean_sec, o))
+            return c
+
+        lax.fori_loop(0, n_tile, one, 0)
+
+    def ship_to_helpers(part):
+        mine = flipped(tile)
+        pltpu.make_async_copy(
+            send.at[part, mine],
+            recv.at[part, sec, parity, tile // 2],
+            fr_sem.at[part, sec],
+        ).start()
+
+        def one(k, c):
+            t = lax.rem(tile + k, n_tile)
+            ship(part, flipped(t), (sec, t))
+            return c
+
+        lax.fori_loop(1, n_tile, one, 0)
+
+    def spread(number, part, a):
+        pltpu.make_async_copy(recv.at[part, a], recv.at[part, a], fr_sem.at[part, a]).wait()
+        hi, lo = split(recv[part, a].reshape(n_tile * cap, width))
+        return matmul(smat[number], hi) + matmul(smat[number], lo)
+
+    def partial_copy():
+        return pltpu.make_async_remote_copy(
+            src_ref=mine_sum,
+            dst_ref=far_sum.at[sec],
+            send_sem=ps_sem,
+            recv_sem=pr_sem.at[sec],
+            device_id=(ocean_sec, flipped(tile)),
+            device_id_type=pl.DeviceIdType.MESH,
+        )
 
     @pl.when(jnp.logical_not(is_ocean))
     def _():
-        f0, f1 = fo[0, 0], fo[0, 1]
-        phi, plo = split(jnp.concatenate([f0, f0 - f1], axis=0))
-        pall = jnp.concatenate([phi, plo], axis=0)
-        for t in range(ntab):
-            r = matmul(pall, thi[t])
-            r = r[: 2 * rows] + r[2 * rows :] + matmul(phi, tlo[t])
-            for c in range(2):
-                hi, lo = split(r[c * rows : (c + 1) * rows])
-                pthi[t * rows : (t + 1) * rows, c * width : (c + 1) * width] = hi
-                ptlo[t * rows : (t + 1) * rows, c * width : (c + 1) * width] = lo
-        out = matmul(mmat[...], pthi[...]) + matmul(mmat[...], ptlo[...])
-        send[...] = out.reshape(send.shape)
-
-        def ship(k, c):
-            o = lax.rem(tile + k, n_tile)
-            pltpu.make_async_remote_copy(
-                src_ref=send.at[o],
-                dst_ref=recv.at[sec, parity, tile // 2],
-                send_sem=fs_sem,
-                recv_sem=fr_sem.at[sec],
-                device_id=(ocean_sec, o),
-                device_id_type=pl.DeviceIdType.MESH,
-            ).start()
-            return c
-
-        lax.fori_loop(0, n_tile, ship, 0)
-        for l in range(2, levels):
+        pack(0, fo[0, 0])
+        ship_to_ocean(0)
+        for l in range(1, levels):
             fo[0, l] = stencil(l)
+        pack(1, fo[0, 0] - fo[0, 1])
+
+        @pl.when(is_near)
+        def _():
+            ship_to_ocean(1)
+
+        @pl.when(is_far)
+        def _():
+            ship_to_helpers(1)
+
         for t in range(ntab):
             hi, lo = split(tab[t].T)
             tthi[t] = hi
             ttlo[t] = lo
+
+        @pl.when(is_far)
+        def _():
+            mine_sum[...] = spread(0, 1, sec)
+            partial_copy().start()
+
         pltpu.make_async_copy(arr, arr, br_sem).wait()
         uhi, ulo = split(arr[...].reshape(n_tile * cap, width))
         v = matmul(mtmat[...], uhi) + matmul(mtmat[...], ulo)
@@ -277,28 +358,37 @@
             r = matmul(jnp.concatenate([vhi, vlo], axis=0), tthi[t])
             total = total + r[:rows] + r[rows:] + matmul(vhi, ttlo[t])
         su[0] = total
-        pltpu.make_async_copy(send, send, fs_sem).wait()
+        pltpu.make_async_copy(send.at[0], send.at[0], fs_sem.at[0]).wait()
+
+        @pl.when(is_near)
+        def _():
+            pltpu.make_async_copy(send.at[1], send.at[1], fs_sem.at[1]).wait()
+
+        @pl.when(is_far)
+        def _():
+            others = send.at[1, 1:n_tile]
+            pltpu.make_async_copy(others, others, fs_sem.at[1]).wait()
+            partial_copy().wait_send()
+
 
     @pl.when(is_ocean)
     def _():
-        for l in range(2, levels):
+        for l in range(1, levels):
             fo[0, l] = stencil(l)
-        flux = jnp.zeros((rows, 2 * width), F32)
-        for a in range(n_atm):
-            pltpu.make_async_copy(recv.at[a], recv.at[a], fr_sem.at[a]).wait()
-            hi, lo = split(recv[a].reshape(n_tile * cap, 2 * width))
-            flux = flux + matmul(smat[a], hi) + matmul(smat[a], lo)
         water = mask[...].astype(F32)
-        first = fo[0, 0] + forcing_rate * water * flux[:, :width]
-        second = fo[0, 1] + forcing_rate * water * flux[:, width:]
+        flux = spread(near_sec, 0, near_sec)
+        for a in range(near_sec):
+            flux = flux + spread(a, 0, a)
+        first = fo[0, 0] + forcing_rate * water * flux
         sea = water * first
         hi, lo = split(sea)
         both = jnp.concatenate([hi, lo], axis=0)
         for a in range(n_atm):
             ret[a] = matmul(rmat[a], both).reshape(ret.shape[1:])
 
-            def back(k, c):
-                t = lax.rem(tile + k, n_tile)
+        def back(k, c):
+            t = lax.rem(tile + k, n_tile)
+            for a in range(n_atm):
                 pltpu.make_async_remote_copy(
                     src_ref=ret.at[a, lax.rem(t, 2), t // 2],
                     dst_ref=arr.at[tile],
@@ -307,12 +397,16 @@
                     device_id=(a, t),
                     device_id_type=pl.DeviceIdType.MESH,
                 ).start()
-                return c
-
-            lax.fori_loop(0, n_tile, back, 0)
+            return c
+
+        lax.fori_loop(0, n_tile, back, 0)
         fo[0, 0] = first
-        fo[0, 1] = second
         su[0] = sea
+        flux = spread(near_sec, 1, near_sec)
+        for a in range(near_sec):
+            pltpu.make_async_copy(far_sum.at[a], far_sum.at[a], pr_sem.at[a]).wait()
+            flux = flux + far_sum[a]
+        fo[0, 1] = fo[0, 1] + forcing_rate * water * flux
         pltpu.make_async_copy(ret, ret, bs_sem).wait()
 
 
@@ -330,7 +424,6 @@
     scratch = [
         pltpu.VMEM((levels, padded, width), F32),
         pltpu.VMEM((2, padded, width), F32),
-        pltpu.VMEM((levels, padded, width), F32),
         pltpu.VMEM((fan_out, blocks), jnp.int32),
         pltpu.VMEM((fan_out, blocks), jnp.int32),
         pltpu.VMEM((fan_out, blocks), jnp.int32),
@@ -344,33 +437,38 @@
         pltpu.VMEM((ntab, width, width), BF16),
         pltpu.VMEM((slots, ntab * rows), BF16),
         pltpu.VMEM((ntab * rows, slots), BF16),
-        pltpu.VMEM((ntab * rows, 2 * width), BF16),
-        pltpu.VMEM((ntab * rows, 2 * width), BF16),
-        pltpu.VMEM((n_tile, cap, 2 * width), F32),
-        pltpu.VMEM((n_atm, 2, half, cap, 2 * width), F32),
-        pltpu.VMEM((n_atm * half, 2 * rows), F32),
-        pltpu.VMEM((n_atm * half, 2 * rows), F32),
-        pltpu.VMEM((n_atm * half, 2 * rows), F32),
-        pltpu.VMEM((n_atm * half, 2 * rows), F32),
+        pltpu.VMEM((ntab * rows, width), BF16),
+        pltpu.VMEM((ntab * rows, width), BF16),
+        pltpu.VMEM((2, n_tile, cap, width), F32),
+        pltpu.VMEM((2, n_atm, 2, half, cap, width), F32),
+        pltpu.VMEM((half, 2 * rows), F32),
+        pltpu.VMEM((half, 2 * rows), F32),
+        pltpu.VMEM((half, 2 * rows), F32),
+        pltpu.VMEM((half, 2 * rows), F32),
         pltpu.VMEM((n_atm, rows, slots), BF16),
         pltpu.VMEM((n_atm, slots, 2 * rows), BF16),
         pltpu.VMEM((n_atm, 2, half, cap, width), F32),
         pltpu.VMEM((n_tile, cap, width), F32),
+        pltpu.VMEM((rows, width), F32),
+        pltpu.VMEM((n_atm - 1, rows, width), F32),
         pltpu.SemaphoreType.DMA((7,)),
         pltpu.SemaphoreType.DMA((2,)),
         pltpu.SemaphoreType.DMA((2,)),
-        pltpu.SemaphoreType.DMA,
-        pltpu.SemaphoreType.DMA((n_atm,)),
+        pltpu.SemaphoreType.DMA((2,)),
+        pltpu.SemaphoreType.DMA((2, n_atm)),
         pltpu.SemaphoreType.DMA,
         pltpu.SemaphoreType.DMA,
+        pltpu.SemaphoreType.DMA,
+        pltpu.SemaphoreType.DMA((n_atm - 1,)),
     ]
+    operands = (fields, coefficients, owner_tile.T, dest_block.T, table_index.T, tables, land_mask)
     return pl.pallas_call(
         functools.partial(kernel, n_sec, n_tile, cap),
         out_shape=(
             jax.ShapeDtypeStruct(fields.shape, F32),
             jax.ShapeDtypeStruct((1, rows, width), F32),
         ),
-        in_specs=[pl.BlockSpec(memory_space=pl.ANY)] * 7,
+        in_specs=[pl.BlockSpec(memory_space=pltpu.HBM)] * 7,
         out_specs=(
             pl.BlockSpec(memory_space=pltpu.VMEM),
             pl.BlockSpec(memory_space=pltpu.VMEM),
@@ -379,7 +477,7 @@
         compiler_params=pltpu.CompilerParams(
             collective_id=0, has_side_effects=True, vmem_limit_bytes=32 * 1024 * 1024
         ),
-    )(fields, coefficients, owner_tile.T, dest_block.T, table_index.T, tables, land_mask)
+    )(*(pltpu.with_memory_space_constraint(x, pltpu.HBM) for x in operands))
 
 
 def solution(mesh):

time: 48.1 us -> 35.2 us (0.73)
  local copies, waits for them, and re-layouts: 7.64 us -> 1.33 us
  Pallas kernels: 39.4 us -> 33.1 us
    unnamed x16 -> x2, local copies, waits for them, and re-layouts: 7.64 us -> 1.33 us
    pallas_call x1, Pallas kernels: 39.4 us -> 33.1 us  [local(): pl.pallas_call(functools.partial(kernel, n_sec, n_tile, cap), out_shape=(...]
where the time goes in v2:
time: 35.2 us; the launch traced here: 35 us
  Pallas kernels  33.1 us (94%)
  local copies, waits for them, and re-layouts  1.33 us (4%)
  between operations  0.64 us (2%)
    pallas_call x1, Pallas kernels, local(): pl.pallas_call(functools.partial(kernel, n_sec, n_tile, cap), out_shape=(...  33.1 us
    unnamed x2, local copies, waits for them, and re-layouts  1.33 us

profile of v2, /device:TPU:1, one launch (start us, length us, event | category | flops | bytes accessed | tf_op | source)
XLA Modules:
  0.0 35.0 jit_solution(13997333764178782110)
XLA Ops:
  0.6 33.1 %shard_map.86 = (f32[1,4,64,256]{3,2,1,0:T(8,128)S(1)}, f32[1,64,256]{2,1,0:T(8,128)S(1)}) custom-call(f32[1,4,64,256]{3,2,1,0:T(8,128)} %fields.1, f32[1,2,64,256]{3,2,1,0:T(8,128)} %coef.1, s32[2,6144]{1,0:T(2,128)} %bitcast.3, s32[2,6144]{1,0:T(2,128)} %bitcast.4, s32[2,6144]{1,0:T(2,128)} %bitcast.5, f32[4,256,256]{2,1,0:T(8,128)} %tables.1, ...), custom_call_target="tpu_custom_call" | custom-call | tf_op jit(solution)/shard_map/pallas_call | solution.py:465
  33.7 0.7 %copy.11 = f32[1,4,64,256]{3,2,1,0:T(8,128)} copy(f32[1,4,64,256]{3,2,1,0:T(8,128)S(1)} %get-tuple-element.4) | data formatting | bytes 524288
  34.4 0.6 %copy.12 = f32[1,64,256]{2,1,0:T(8,128)} copy(f32[1,64,256]{2,1,0:T(8,128)S(1)} %get-tuple-element.5) | data formatting | bytes 131072

commit v3 on v2

--- a/solution.py
+++ b/solution.py
@@ -34,7 +34,7 @@
     ext, cext, ot, db, ti, tab, mask, hsend, hrecv,
     thi, tlo, tthi, ttlo, mmat, mtmat, pthi, ptlo, send, recv,
     x0, x1, d0, d1, smat, rmat, ret, arr, mine_sum, far_sum,
-    in_sem, hs_sem, hr_sem, fs_sem, fr_sem, bs_sem, br_sem, ps_sem, pr_sem,
+    in_sem, hs_sem, hr_sem, fs_sem, fr_sem, bs_sem, br_sem, ps_sem, pr_sem, z_sem, x_sem,
 ):
     n_atm = n_sec - 1
     ocean_sec = n_sec - 1
@@ -73,35 +73,25 @@
 
     barrier = pltpu.get_barrier_semaphore()
 
-    def greet(s, t):
-        pl.semaphore_signal(barrier, inc=1, device_id=(s, t), device_id_type=pl.DeviceIdType.MESH)
-
-    def greet_tiles(s, first):
-        def one(k, c):
-            greet(s, lax.rem(tile + k, n_tile))
-            return c
-
-        lax.fori_loop(first, n_tile, one, 0)
-
-    @pl.when(is_ocean)
-    def _():
-        for a in range(n_atm):
-            greet_tiles(a, 0)
-        greet(sec, upper)
-        greet(sec, lower)
-
-    @pl.when(jnp.logical_not(is_ocean))
-    def _():
-        greet_tiles(ocean_sec, 0)
-
-    @pl.when(is_far)
-    def _():
-        greet_tiles(sec, 1)
-
-    @pl.when(is_near)
-    def _():
-        greet(sec, upper)
-        greet(sec, lower)
+    def greet(semaphore, s, t):
+        pl.semaphore_signal(semaphore, inc=1, device_id=(s, t), device_id_type=pl.DeviceIdType.MESH)
+
+    def z_ring(semaphore):
+        for k in range(1, 4):
+            greet(semaphore, sec, lax.rem(tile + 8 * k, n_tile))
+
+    def x_ring(semaphore):
+        for k in range(1, 4):
+            greet(semaphore, sec, (tile // 8) * 8 + lax.rem(lax.rem(tile, 8) + 2 * k, 8))
+
+    for k in range(1, n_sec):
+        s = lax.rem(sec + k, n_sec)
+        greet(barrier, s, tile)
+        greet(barrier, s, flipped(tile))
+    greet(barrier, sec, flipped(tile))
+    greet(barrier, sec, jnp.where(parity == 0, upper, lower))
+    z_ring(barrier)
+    x_ring(barrier)
 
     zero = jnp.zeros((PAD, width), F32)
     for l in range(levels):
@@ -120,17 +110,7 @@
         hsend[0, 8 + c : 9 + c, :] = cext[c, top : top + 1, :]
         hsend[1, 8 + c : 9 + c, :] = cext[c, low - 1 : low, :]
 
-    @pl.when(is_ocean)
-    def _():
-        pl.semaphore_wait(barrier, 2 + n_atm * n_tile)
-
-    @pl.when(is_far)
-    def _():
-        pl.semaphore_wait(barrier, n_tile - 1 + n_tile)
-
-    @pl.when(is_near)
-    def _():
-        pl.semaphore_wait(barrier, 2 + n_tile)
+    pl.semaphore_wait(barrier, 2 * n_sec + 6)
 
     def halo(way, to):
         return pltpu.make_async_remote_copy(
@@ -145,6 +125,8 @@
     halos = [halo(0, upper), halo(1, lower)]
     for copy in halos:
         copy.start()
+
+    z_ring(z_sem)
 
     loads[2].wait()
     loads[3].wait()
@@ -239,6 +221,9 @@
             thi[t] = hi
             tlo[t] = lo
 
+    pl.semaphore_wait(z_sem, 3)
+    x_ring(x_sem)
+
     for copy in halos:
         copy.wait()
     above = jnp.where(tile > 0, hrecv[0], 0.0)
@@ -326,6 +311,7 @@
     @pl.when(jnp.logical_not(is_ocean))
     def _():
         pack(0, fo[0, 0])
+        pl.semaphore_wait(x_sem, 3)
         ship_to_ocean(0)
         for l in range(1, levels):
             fo[0, l] = stencil(l)
@@ -373,6 +359,7 @@
 
     @pl.when(is_ocean)
     def _():
+        pl.semaphore_wait(x_sem, 3)
         for l in range(1, levels):
             fo[0, l] = stencil(l)
         water = mask[...].astype(F32)
@@ -386,20 +373,26 @@
         for a in range(n_atm):
             ret[a] = matmul(rmat[a], both).reshape(ret.shape[1:])
 
-        def back(k, c):
-            t = lax.rem(tile + k, n_tile)
-            for a in range(n_atm):
-                pltpu.make_async_remote_copy(
-                    src_ref=ret.at[a, lax.rem(t, 2), t // 2],
-                    dst_ref=arr.at[tile],
-                    send_sem=bs_sem,
-                    recv_sem=br_sem,
-                    device_id=(a, t),
-                    device_id_type=pl.DeviceIdType.MESH,
-                ).start()
-            return c
-
-        lax.fori_loop(0, n_tile, back, 0)
+        def back(sections):
+            def one(k, c):
+                i = lax.rem(k, 16)
+                j = i // 2
+                z = 2 * (k // 16) + lax.rem(i + tile // 8, 2)
+                t = 8 * z + 2 * lax.rem(j + tile // 2, 4) + j // 4
+                for a in sections:
+                    pltpu.make_async_remote_copy(
+                        src_ref=ret.at[a, lax.rem(t, 2), t // 2],
+                        dst_ref=arr.at[tile],
+                        send_sem=bs_sem,
+                        recv_sem=br_sem,
+                        device_id=(a, t),
+                        device_id_type=pl.DeviceIdType.MESH,
+                    ).start()
+                return c
+
+            lax.fori_loop(0, n_tile, one, 0)
+
+        back((1, 0, 2))
         fo[0, 0] = first
         su[0] = sea
         flux = spread(near_sec, 1, near_sec)
@@ -408,6 +401,17 @@
             flux = flux + far_sum[a]
         fo[0, 1] = fo[0, 1] + forcing_rate * water * flux
         pltpu.make_async_copy(ret, ret, bs_sem).wait()
+
+
+def store(fields, surface, fields_out, surface_out, sems):
+    copies = [
+        pltpu.make_async_copy(fields, fields_out, sems.at[0]),
+        pltpu.make_async_copy(surface, surface_out, sems.at[1]),
+    ]
+    for copy in copies:
+        copy.start()
+    for copy in copies:
+        copy.wait()
 
 
 def local(fields, coefficients, owner_tile, dest_block, table_index, tables, land_mask):
@@ -460,14 +464,17 @@
         pltpu.SemaphoreType.DMA,
         pltpu.SemaphoreType.DMA,
         pltpu.SemaphoreType.DMA((n_atm - 1,)),
+        pltpu.SemaphoreType.REGULAR,
+        pltpu.SemaphoreType.REGULAR,
     ]
     operands = (fields, coefficients, owner_tile.T, dest_block.T, table_index.T, tables, land_mask)
-    return pl.pallas_call(
+    shapes = (
+        jax.ShapeDtypeStruct(fields.shape, F32),
+        jax.ShapeDtypeStruct((1, rows, width), F32),
+    )
+    results = pl.pallas_call(
         functools.partial(kernel, n_sec, n_tile, cap),
-        out_shape=(
-            jax.ShapeDtypeStruct(fields.shape, F32),
-            jax.ShapeDtypeStruct((1, rows, width), F32),
-        ),
+        out_shape=shapes,
         in_specs=[pl.BlockSpec(memory_space=pltpu.HBM)] * 7,
         out_specs=(
             pl.BlockSpec(memory_space=pltpu.VMEM),
@@ -478,6 +485,13 @@
             collective_id=0, has_side_effects=True, vmem_limit_bytes=32 * 1024 * 1024
         ),
     )(*(pltpu.with_memory_space_constraint(x, pltpu.HBM) for x in operands))
+    return pl.pallas_call(
+        store,
+        out_shape=shapes,
+        in_specs=[pl.BlockSpec(memory_space=pltpu.VMEM)] * 2,
+        out_specs=(pl.BlockSpec(memory_space=pl.ANY),) * 2,
+        scratch_shapes=[pltpu.SemaphoreType.DMA((2,))],
+    )(*(pltpu.with_memory_space_constraint(x, pltpu.VMEM) for x in results))
 
 
 def solution(mesh):

time: 35.2 us -> 31.4 us (0.89)
  Pallas kernels: 33.1 us -> 30.6 us
  local copies, waits for them, and re-layouts: 1.33 us -> 0 us
    pallas_call x1 -> x2, Pallas kernels: 33.1 us -> 30.6 us  [the longest x1 29.9 us: local(): pl.pallas_call(functools.partial(kernel, n_sec, n_tile, cap), out_shape=s...]
    unnamed x2 -> x0, local copies, waits for them, and re-layouts: 1.33 us -> none
where the time goes in v3:
time: 31.4 us; the launch traced here: 31.2 us
  Pallas kernels  30.6 us (97%)
  between operations  0.64 us (2%)
    pallas_call x1, Pallas kernels, local(): pl.pallas_call(functools.partial(kernel, n_sec, n_tile, cap), out_shape=s...  29.9 us
    pallas_call x1, Pallas kernels, local(): pl.pallas_call(store, out_shape=shapes, in_specs=[pl.BlockSpec(memory_spa...  0.74 us

profile of v3, /device:TPU:1, one launch (start us, length us, event | category | flops | bytes accessed | tf_op | source)
XLA Modules:
  0.0 31.2 jit_solution(8651661524806703061)
XLA Ops:
  0.6 29.9 %shard_map.86 = (f32[1,4,64,256]{3,2,1,0:T(8,128)S(1)}, f32[1,64,256]{2,1,0:T(8,128)S(1)}) custom-call(f32[1,4,64,256]{3,2,1,0:T(8,128)} %fields.1, f32[1,2,64,256]{3,2,1,0:T(8,128)} %coef.1, s32[2,6144]{1,0:T(2,128)} %bitcast.3, s32[2,6144]{1,0:T(2,128)} %bitcast.4, s32[2,6144]{1,0:T(2,128)} %bitcast.5, f32[4,256,256]{2,1,0:T(8,128)} %tables.1, ...), custom_call_target="tpu_custom_call" | custom-call | tf_op jit(solution)/shard_map/pallas_call | solution.py:475
  30.5 0.7 %shard_map.87 = (f32[1,4,64,256]{3,2,1,0:T(8,128)}, f32[1,64,256]{2,1,0:T(8,128)}) custom-call(f32[1,4,64,256]{3,2,1,0:T(8,128)S(1)} %get-tuple-element.4.fields, f32[1,64,256]{2,1,0:T(8,128)S(1)} %get-tuple-element.5.surface), custom_call_target="tpu_custom_call" | custom-call | tf_op jit(solution)/shard_map/pallas_call | solution.py:488

commit v4 on v3

--- a/solution.py
+++ b/solution.py
@@ -33,12 +33,13 @@
     fo, su,
     ext, cext, ot, db, ti, tab, mask, hsend, hrecv,
     thi, tlo, tthi, ttlo, mmat, mtmat, pthi, ptlo, send, recv,
-    x0, x1, d0, d1, smat, rmat, ret, arr, mine_sum, far_sum,
-    in_sem, hs_sem, hr_sem, fs_sem, fr_sem, bs_sem, br_sem, ps_sem, pr_sem, z_sem, x_sem,
+    x0, x1, d0, d1, smat, rmat, ret, arr, mine_sum, far_sum, base, flux0, far_mask,
+    in_sem, hs_sem, hr_sem, fs_sem, fr_sem, bs_sem, br_sem, ps_sem, pr_sem, z_sem, cs_sem, cr_sem,
 ):
     n_atm = n_sec - 1
     ocean_sec = n_sec - 1
     near_sec = n_sec - 2
+    relay_sec = near_sec - 1
     half = n_tile // 2
     levels, rows, width = fo.shape[1:]
     ntab = tables.shape[0]
@@ -50,6 +51,7 @@
     is_ocean = sec == ocean_sec
     is_near = sec == near_sec
     is_far = sec < near_sec
+    is_relay = sec == relay_sec
     parity = lax.rem(tile, 2)
 
     def flipped(t):
@@ -76,13 +78,14 @@
     def greet(semaphore, s, t):
         pl.semaphore_signal(semaphore, inc=1, device_id=(s, t), device_id_type=pl.DeviceIdType.MESH)
 
-    def z_ring(semaphore):
-        for k in range(1, 4):
-            greet(semaphore, sec, lax.rem(tile + 8 * k, n_tile))
-
-    def x_ring(semaphore):
-        for k in range(1, 4):
-            greet(semaphore, sec, (tile // 8) * 8 + lax.rem(lax.rem(tile, 8) + 2 * k, 8))
+    def plane(semaphore):
+        def one(k, c):
+            z = lax.rem(tile // 8 + k // 4, 4)
+            x = lax.rem(tile // 2 + lax.rem(k, 4), 4)
+            greet(semaphore, sec, z * 8 + x * 2 + parity)
+            return c
+
+        lax.fori_loop(1, n_tile // 2, one, 0)
 
     for k in range(1, n_sec):
         s = lax.rem(sec + k, n_sec)
@@ -90,8 +93,7 @@
         greet(barrier, s, flipped(tile))
     greet(barrier, sec, flipped(tile))
     greet(barrier, sec, jnp.where(parity == 0, upper, lower))
-    z_ring(barrier)
-    x_ring(barrier)
+    plane(barrier)
 
     zero = jnp.zeros((PAD, width), F32)
     for l in range(levels):
@@ -110,7 +112,26 @@
         hsend[0, 8 + c : 9 + c, :] = cext[c, top : top + 1, :]
         hsend[1, 8 + c : 9 + c, :] = cext[c, low - 1 : low, :]
 
-    pl.semaphore_wait(barrier, 2 * n_sec + 6)
+    pl.semaphore_wait(barrier, 2 * n_sec + n_tile // 2 - 1)
+
+    def column_copy(src, dst, number, to):
+        return pltpu.make_async_remote_copy(
+            src_ref=src,
+            dst_ref=dst,
+            send_sem=cs_sem.at[number],
+            recv_sem=cr_sem.at[number],
+            device_id=(to, flipped(tile)),
+            device_id_type=pl.DeviceIdType.MESH,
+        )
+
+    def mask_copy():
+        return column_copy(mask, far_mask, 0, relay_sec)
+
+    def base_copy():
+        return column_copy(base, base, 1, relay_sec)
+
+    def flux_copy():
+        return column_copy(flux0, flux0, 2, ocean_sec)
 
     def halo(way, to):
         return pltpu.make_async_remote_copy(
@@ -126,13 +147,22 @@
     for copy in halos:
         copy.start()
 
-    z_ring(z_sem)
+    @pl.when(is_ocean)
+    def _():
+        loads[6].wait()
+        mask_copy().start()
+
+    plane(z_sem)
 
     loads[2].wait()
     loads[3].wait()
     loads[4].wait()
     loads[5].wait()
-    loads[6].wait()
+
+    @pl.when(jnp.logical_not(is_ocean))
+    def _():
+        loads[6].wait()
+
 
     lane = iota((8, 128), 1)
     left = lane < 64
@@ -177,12 +207,16 @@
 
     @pl.when(is_ocean)
     def _():
+        place(near_sec, near_sec, tile)
+
+    @pl.when(is_relay)
+    def _():
         for a in range(n_atm):
-            place(a, a, tile)
-
-    @pl.when(is_far)
-    def _():
-        place(0, sec, flipped(tile))
+            place(a, a, flipped(tile))
+
+    @pl.when(sec < relay_sec)
+    def _():
+        place(0, 0, flipped(tile))
 
     @pl.when(jnp.logical_not(is_ocean))
     def _():
@@ -221,9 +255,6 @@
             thi[t] = hi
             tlo[t] = lo
 
-    pl.semaphore_wait(z_sem, 3)
-    x_ring(x_sem)
-
     for copy in halos:
         copy.wait()
     above = jnp.where(tile > 0, hrecv[0], 0.0)
@@ -260,43 +291,69 @@
         out = matmul(mmat[...], pthi[...]) + matmul(mmat[...], ptlo[...])
         send[part] = out.reshape(send.shape[1:])
 
-    def ship(part, o, to):
-        pltpu.make_async_remote_copy(
-            src_ref=send.at[part, o],
-            dst_ref=recv.at[part, sec, parity, tile // 2],
-            send_sem=fs_sem.at[part],
-            recv_sem=fr_sem.at[part, sec],
-            device_id=to,
-            device_id_type=pl.DeviceIdType.MESH,
-        ).start()
-
-    def ship_to_ocean(part):
-        def one(k, c):
-            o = lax.rem(tile + k, n_tile)
-            ship(part, o, (ocean_sec, o))
-            return c
-
-        lax.fori_loop(0, n_tile, one, 0)
-
-    def ship_to_helpers(part):
-        mine = flipped(tile)
-        pltpu.make_async_copy(
-            send.at[part, mine],
-            recv.at[part, sec, parity, tile // 2],
-            fr_sem.at[part, sec],
-        ).start()
-
+    def ship(part, to, whole):
         def one(k, c):
             t = lax.rem(tile + k, n_tile)
-            ship(part, flipped(t), (sec, t))
+            o = t if to == ocean_sec else flipped(t)
+            pltpu.make_async_remote_copy(
+                src_ref=send.at[part, o],
+                dst_ref=recv.at[part, sec, parity, tile // 2],
+                send_sem=fs_sem.at[part],
+                recv_sem=fr_sem.at[part, sec],
+                device_id=(to, t),
+                device_id_type=pl.DeviceIdType.MESH,
+            ).start()
             return c
 
-        lax.fori_loop(1, n_tile, one, 0)
+        if not whole:
+            pltpu.make_async_copy(
+                send.at[part, flipped(tile)],
+                recv.at[part, sec, parity, tile // 2],
+                fr_sem.at[part, sec],
+            ).start()
+        lax.fori_loop(0 if whole else 1, n_tile, one, 0)
+
+    def shipped(part, whole):
+        sent = send.at[part, (0 if whole else 1) : n_tile]
+        pltpu.make_async_copy(sent, sent, fs_sem.at[part]).wait()
 
     def spread(number, part, a):
         pltpu.make_async_copy(recv.at[part, a], recv.at[part, a], fr_sem.at[part, a]).wait()
         hi, lo = split(recv[part, a].reshape(n_tile * cap, width))
         return matmul(smat[number], hi) + matmul(smat[number], lo)
+
+    def give_back():
+        ocean_tile = flipped(tile)
+
+        def one(k, c):
+            i = lax.rem(k, 16)
+            j = i // 2
+            z = 2 * (k // 16) + lax.rem(i + tile // 8, 2)
+            t = 8 * z + 2 * lax.rem(j + tile // 2, 4) + j // 4
+
+            def to(a):
+                return pltpu.make_async_remote_copy(
+                    src_ref=ret.at[a * n_tile + lax.rem(t, 2) * half + t // 2],
+                    dst_ref=arr.at[ocean_tile],
+                    send_sem=bs_sem,
+                    recv_sem=br_sem,
+                    device_id=(a, t),
+                    device_id_type=pl.DeviceIdType.MESH,
+                )
+
+            @pl.when(t != tile)
+            def _():
+                to(relay_sec).start()
+
+            for a in range(n_atm):
+                if a != relay_sec:
+                    to(a).start()
+            return c
+
+        lax.fori_loop(0, n_tile, one, 0)
+        pltpu.make_async_copy(
+            ret.at[relay_sec * n_tile + parity * half + tile // 2], arr.at[ocean_tile], br_sem
+        ).start()
 
     def partial_copy():
         return pltpu.make_async_remote_copy(
@@ -311,28 +368,55 @@
     @pl.when(jnp.logical_not(is_ocean))
     def _():
         pack(0, fo[0, 0])
-        pl.semaphore_wait(x_sem, 3)
-        ship_to_ocean(0)
+        pl.semaphore_wait(z_sem, n_tile // 2 - 1)
+
+        @pl.when(is_relay)
+        def _():
+            ship(0, relay_sec, False)
+
+        @pl.when(jnp.logical_not(is_relay))
+        def _():
+            ship(0, relay_sec, True)
+
         for l in range(1, levels):
             fo[0, l] = stencil(l)
         pack(1, fo[0, 0] - fo[0, 1])
 
         @pl.when(is_near)
         def _():
-            ship_to_ocean(1)
-
-        @pl.when(is_far)
-        def _():
-            ship_to_helpers(1)
+            ship(1, ocean_sec, True)
+
+        for a in range(near_sec):
+
+            @pl.when(sec == a)
+            def _():
+                ship(1, a, False)
+
 
         for t in range(ntab):
             hi, lo = split(tab[t].T)
             tthi[t] = hi
             ttlo[t] = lo
 
+        @pl.when(is_relay)
+        def _():
+            mask_copy().wait_recv()
+            base_copy().wait_recv()
+            water = far_mask[...].astype(F32)
+            flux = spread(near_sec, 0, near_sec)
+            for a in (1, 0):
+                flux = flux + spread(a, 0, a)
+            flux0[...] = flux
+            flux_copy().start()
+            hi, lo = split(water * (base[...] + forcing_rate * water * flux))
+            both = jnp.concatenate([hi, lo], axis=0)
+            for a in range(n_atm):
+                ret[a * n_tile : (a + 1) * n_tile] = matmul(rmat[a], both).reshape(n_tile, cap, width)
+            give_back()
+
         @pl.when(is_far)
         def _():
-            mine_sum[...] = spread(0, 1, sec)
+            mine_sum[...] = spread(sec, 1, sec)
             partial_copy().start()
 
         pltpu.make_async_copy(arr, arr, br_sem).wait()
@@ -344,63 +428,47 @@
             r = matmul(jnp.concatenate([vhi, vlo], axis=0), tthi[t])
             total = total + r[:rows] + r[rows:] + matmul(vhi, ttlo[t])
         su[0] = total
-        pltpu.make_async_copy(send.at[0], send.at[0], fs_sem.at[0]).wait()
+
+        @pl.when(is_relay)
+        def _():
+            shipped(0, False)
+            others = ret.at[1 : n_atm * n_tile]
+            pltpu.make_async_copy(others, others, bs_sem).wait()
+            flux_copy().wait_send()
+
+        @pl.when(jnp.logical_not(is_relay))
+        def _():
+            shipped(0, True)
 
         @pl.when(is_near)
         def _():
-            pltpu.make_async_copy(send.at[1], send.at[1], fs_sem.at[1]).wait()
+            shipped(1, True)
 
         @pl.when(is_far)
         def _():
-            others = send.at[1, 1:n_tile]
-            pltpu.make_async_copy(others, others, fs_sem.at[1]).wait()
+            shipped(1, False)
             partial_copy().wait_send()
 
 
     @pl.when(is_ocean)
     def _():
-        pl.semaphore_wait(x_sem, 3)
+        base[...] = fo[0, 0]
+        base_copy().start()
+        pl.semaphore_wait(z_sem, n_tile // 2 - 1)
         for l in range(1, levels):
             fo[0, l] = stencil(l)
         water = mask[...].astype(F32)
-        flux = spread(near_sec, 0, near_sec)
-        for a in range(near_sec):
-            flux = flux + spread(a, 0, a)
-        first = fo[0, 0] + forcing_rate * water * flux
-        sea = water * first
-        hi, lo = split(sea)
-        both = jnp.concatenate([hi, lo], axis=0)
-        for a in range(n_atm):
-            ret[a] = matmul(rmat[a], both).reshape(ret.shape[1:])
-
-        def back(sections):
-            def one(k, c):
-                i = lax.rem(k, 16)
-                j = i // 2
-                z = 2 * (k // 16) + lax.rem(i + tile // 8, 2)
-                t = 8 * z + 2 * lax.rem(j + tile // 2, 4) + j // 4
-                for a in sections:
-                    pltpu.make_async_remote_copy(
-                        src_ref=ret.at[a, lax.rem(t, 2), t // 2],
-                        dst_ref=arr.at[tile],
-                        send_sem=bs_sem,
-                        recv_sem=br_sem,
-                        device_id=(a, t),
-                        device_id_type=pl.DeviceIdType.MESH,
-                    ).start()
-                return c
-
-            lax.fori_loop(0, n_tile, one, 0)
-
-        back((1, 0, 2))
-        fo[0, 0] = first
-        su[0] = sea
         flux = spread(near_sec, 1, near_sec)
         for a in range(near_sec):
             pltpu.make_async_copy(far_sum.at[a], far_sum.at[a], pr_sem.at[a]).wait()
             flux = flux + far_sum[a]
         fo[0, 1] = fo[0, 1] + forcing_rate * water * flux
-        pltpu.make_async_copy(ret, ret, bs_sem).wait()
+        flux_copy().wait_recv()
+        first = fo[0, 0] + forcing_rate * water * flux0[...]
+        fo[0, 0] = first
+        su[0] = water * first
+        mask_copy().wait_send()
+        base_copy().wait_send()
 
 
 def store(fields, surface, fields_out, surface_out, sems):
@@ -451,10 +519,13 @@
         pltpu.VMEM((half, 2 * rows), F32),
         pltpu.VMEM((n_atm, rows, slots), BF16),
         pltpu.VMEM((n_atm, slots, 2 * rows), BF16),
-        pltpu.VMEM((n_atm, 2, half, cap, width), F32),
+        pltpu.VMEM((n_atm * n_tile, cap, width), F32),
         pltpu.VMEM((n_tile, cap, width), F32),
         pltpu.VMEM((rows, width), F32),
         pltpu.VMEM((n_atm - 1, rows, width), F32),
+        pltpu.VMEM((rows, width), F32),
+        pltpu.VMEM((rows, width), F32),
+        pltpu.VMEM((rows, width), jnp.int32),
         pltpu.SemaphoreType.DMA((7,)),
         pltpu.SemaphoreType.DMA((2,)),
         pltpu.SemaphoreType.DMA((2,)),
@@ -465,7 +536,8 @@
         pltpu.SemaphoreType.DMA,
         pltpu.SemaphoreType.DMA((n_atm - 1,)),
         pltpu.SemaphoreType.REGULAR,
-        pltpu.SemaphoreType.REGULAR,
+        pltpu.SemaphoreType.DMA((3,)),
+        pltpu.SemaphoreType.DMA((3,)),
     ]
     operands = (fields, coefficients, owner_tile.T, dest_block.T, table_index.T, tables, land_mask)
     shapes = (

time: 31.4 us -> 29.4 us (0.936)
  Pallas kernels: 30.6 us -> 28.6 us
    pallas_call x1, Pallas kernels: 29.9 us -> 27.9 us  [local(): pl.pallas_call(functools.partial(kernel, n_sec, n_tile, cap), out_shape=s...]
where the time goes in v4:
time: 29.4 us; the launch traced here: 29.3 us
  Pallas kernels  28.6 us (97%)
  between operations  0.64 us (2%)
    pallas_call x1, Pallas kernels, local(): pl.pallas_call(functools.partial(kernel, n_sec, n_tile, cap), out_shape=s...  27.9 us
    pallas_call x1, Pallas kernels, local(): pl.pallas_call(store, out_shape=shapes, in_specs=[pl.BlockSpec(memory_spa...  0.74 us

profile of v4, /device:TPU:1, one launch (start us, length us, event | category | flops | bytes accessed | tf_op | source)
XLA Modules:
  0.0 29.3 jit_solution(16848329916233113978)
XLA Ops:
  0.6 27.9 %shard_map.86 = (f32[1,4,64,256]{3,2,1,0:T(8,128)S(1)}, f32[1,64,256]{2,1,0:T(8,128)S(1)}) custom-call(f32[1,4,64,256]{3,2,1,0:T(8,128)} %fields.1, f32[1,2,64,256]{3,2,1,0:T(8,128)} %coef.1, s32[2,6144]{1,0:T(2,128)} %bitcast.3, s32[2,6144]{1,0:T(2,128)} %bitcast.4, s32[2,6144]{1,0:T(2,128)} %bitcast.5, f32[4,256,256]{2,1,0:T(8,128)} %tables.1, ...), custom_call_target="tpu_custom_call" | custom-call | tf_op jit(solution)/shard_map/pallas_call | solution.py:547
  28.5 0.7 %shard_map.87 = (f32[1,4,64,256]{3,2,1,0:T(8,128)}, f32[1,64,256]{2,1,0:T(8,128)}) custom-call(f32[1,4,64,256]{3,2,1,0:T(8,128)S(1)} %get-tuple-element.4.fields, f32[1,64,256]{2,1,0:T(8,128)S(1)} %get-tuple-element.5.surface), custom_call_target="tpu_custom_call" | custom-call | tf_op jit(solution)/shard_map/pallas_call | solution.py:560

commit v5 on v4

--- a/solution.py
+++ b/solution.py
@@ -33,8 +33,8 @@
     fo, su,
     ext, cext, ot, db, ti, tab, mask, hsend, hrecv,
     thi, tlo, tthi, ttlo, mmat, mtmat, pthi, ptlo, send, recv,
-    x0, x1, d0, d1, smat, rmat, ret, arr, mine_sum, far_sum, base, flux0, far_mask,
-    in_sem, hs_sem, hr_sem, fs_sem, fr_sem, bs_sem, br_sem, ps_sem, pr_sem, z_sem, cs_sem, cr_sem,
+    x0, x1, d0, d1, smat, rmat, ret, arr, base, flux0, far_mask,
+    in_sem, hs_sem, hr_sem, fs_sem, fr_sem, bs_sem, br_sem, o_sem, p_sem, k_sem, b_sem, cs_sem, cr_sem,
 ):
     n_atm = n_sec - 1
     ocean_sec = n_sec - 1
@@ -50,7 +50,6 @@
     lower = lax.rem(tile + 1, n_tile)
     is_ocean = sec == ocean_sec
     is_near = sec == near_sec
-    is_far = sec < near_sec
     is_relay = sec == relay_sec
     parity = lax.rem(tile, 2)
 
@@ -74,26 +73,50 @@
         copy.start()
 
     barrier = pltpu.get_barrier_semaphore()
+    has_upper, has_lower = tile > 0, tile < n_tile - 1
+    neighbours = has_upper.astype(jnp.int32) + has_lower.astype(jnp.int32)
 
     def greet(semaphore, s, t):
         pl.semaphore_signal(semaphore, inc=1, device_id=(s, t), device_id_type=pl.DeviceIdType.MESH)
 
-    def plane(semaphore):
+    @pl.when(jnp.logical_not(has_upper))
+    def _():
+        hrecv[0] = jnp.zeros_like(hrecv[0])
+
+    @pl.when(jnp.logical_not(has_lower))
+    def _():
+        hrecv[1] = jnp.zeros_like(hrecv[1])
+
+    @pl.when(has_upper)
+    def _():
+        greet(barrier, sec, upper)
+
+    @pl.when(has_lower)
+    def _():
+        greet(barrier, sec, lower)
+
+    @pl.when(is_relay | is_ocean)
+    def _():
         def one(k, c):
             z = lax.rem(tile // 8 + k // 4, 4)
             x = lax.rem(tile // 2 + lax.rem(k, 4), 4)
-            greet(semaphore, sec, z * 8 + x * 2 + parity)
+            greet(barrier, sec, z * 8 + x * 2 + parity)
             return c
 
-        lax.fori_loop(1, n_tile // 2, one, 0)
-
-    for k in range(1, n_sec):
-        s = lax.rem(sec + k, n_sec)
-        greet(barrier, s, tile)
-        greet(barrier, s, flipped(tile))
-    greet(barrier, sec, flipped(tile))
-    greet(barrier, sec, jnp.where(parity == 0, upper, lower))
-    plane(barrier)
+        lax.fori_loop(1, half, one, 0)
+
+    @pl.when(is_relay)
+    def _():
+        greet(barrier, ocean_sec, flipped(tile))
+
+    @pl.when(sec == 0)
+    def _():
+        greet(barrier, relay_sec, tile)
+
+    @pl.when(is_near)
+    def _():
+        greet(barrier, ocean_sec, tile)
+        greet(barrier, relay_sec, flipped(tile))
 
     zero = jnp.zeros((PAD, width), F32)
     for l in range(levels):
@@ -103,6 +126,7 @@
         cext[c, 0:top, :] = zero
         cext[c, low : low + PAD, :] = zero
         hsend[c, 8:16, :] = zero
+
     loads[0].wait()
     for l in range(levels):
         hsend[0, 2 * l : 2 * l + 2, :] = ext[l, top : top + 2, :]
@@ -112,7 +136,13 @@
         hsend[0, 8 + c : 9 + c, :] = cext[c, top : top + 1, :]
         hsend[1, 8 + c : 9 + c, :] = cext[c, low - 1 : low, :]
 
-    pl.semaphore_wait(barrier, 2 * n_sec + n_tile // 2 - 1)
+    @pl.when(is_relay | is_ocean)
+    def _():
+        pl.semaphore_wait(barrier, neighbours + half + 1)
+
+    @pl.when(jnp.logical_not(is_relay | is_ocean))
+    def _():
+        pl.semaphore_wait(barrier, neighbours)
 
     def column_copy(src, dst, number, to):
         return pltpu.make_async_remote_copy(
@@ -144,15 +174,23 @@
         )
 
     halos = [halo(0, upper), halo(1, lower)]
-    for copy in halos:
-        copy.start()
+
+    @pl.when(has_upper)
+    def _():
+        halos[0].start()
+
+    @pl.when(has_lower)
+    def _():
+        halos[1].start()
 
     @pl.when(is_ocean)
     def _():
         loads[6].wait()
         mask_copy().start()
 
-    plane(z_sem)
+    @pl.when(is_relay | is_ocean)
+    def _():
+        greet(p_sem, sec, flipped(tile))
 
     loads[2].wait()
     loads[3].wait()
@@ -207,16 +245,13 @@
 
     @pl.when(is_ocean)
     def _():
-        place(near_sec, near_sec, tile)
+        for a in range(n_atm):
+            place(a, a, tile)
 
     @pl.when(is_relay)
     def _():
         for a in range(n_atm):
             place(a, a, flipped(tile))
-
-    @pl.when(sec < relay_sec)
-    def _():
-        place(0, 0, flipped(tile))
 
     @pl.when(jnp.logical_not(is_ocean))
     def _():
@@ -255,10 +290,29 @@
             thi[t] = hi
             tlo[t] = lo
 
-    for copy in halos:
-        copy.wait()
-    above = jnp.where(tile > 0, hrecv[0], 0.0)
-    below = jnp.where(tile < n_tile - 1, hrecv[1], 0.0)
+    @pl.when(is_relay)
+    def _():
+        pl.semaphore_wait(p_sem, 1)
+        greet(k_sem, 0, tile)
+        greet(k_sem, near_sec, flipped(tile))
+
+    @pl.when(is_ocean)
+    def _():
+        pl.semaphore_wait(p_sem, 1)
+        greet(o_sem, near_sec, tile)
+        greet(b_sem, relay_sec, flipped(tile))
+
+    @pl.when(has_upper)
+    def _():
+        halos[0].wait_send()
+        halos[1].wait_recv()
+
+    @pl.when(has_lower)
+    def _():
+        halos[1].wait_send()
+        halos[0].wait_recv()
+
+    above, below = hrecv[0], hrecv[1]
     for l in range(levels):
         ext[l, top - 2 : top, :] = above[2 * l : 2 * l + 2]
         ext[l, low : low + 2, :] = below[2 * l : 2 * l + 2]
@@ -291,12 +345,11 @@
         out = matmul(mmat[...], pthi[...]) + matmul(mmat[...], ptlo[...])
         send[part] = out.reshape(send.shape[1:])
 
-    def ship(part, to, whole):
+    def ship(part, to):
         def one(k, c):
             t = lax.rem(tile + k, n_tile)
-            o = t if to == ocean_sec else flipped(t)
             pltpu.make_async_remote_copy(
-                src_ref=send.at[part, o],
+                src_ref=send.at[part, t if to == ocean_sec else flipped(t)],
                 dst_ref=recv.at[part, sec, parity, tile // 2],
                 send_sem=fs_sem.at[part],
                 recv_sem=fr_sem.at[part, sec],
@@ -305,33 +358,47 @@
             ).start()
             return c
 
-        if not whole:
+        if to == ocean_sec:
+            lax.fori_loop(0, n_tile, one, 0)
+            return
+
+        @pl.when(is_relay)
+        def _():
             pltpu.make_async_copy(
                 send.at[part, flipped(tile)],
                 recv.at[part, sec, parity, tile // 2],
                 fr_sem.at[part, sec],
             ).start()
-        lax.fori_loop(0 if whole else 1, n_tile, one, 0)
-
-    def shipped(part, whole):
-        sent = send.at[part, (0 if whole else 1) : n_tile]
+            lax.fori_loop(1, n_tile, one, 0)
+
+        @pl.when(jnp.logical_not(is_relay))
+        def _():
+            lax.fori_loop(0, n_tile, one, 0)
+
+    def shipped(part, kept):
+        sent = send.at[part, kept:n_tile]
         pltpu.make_async_copy(sent, sent, fs_sem.at[part]).wait()
 
-    def spread(number, part, a):
-        pltpu.make_async_copy(recv.at[part, a], recv.at[part, a], fr_sem.at[part, a]).wait()
-        hi, lo = split(recv[part, a].reshape(n_tile * cap, width))
-        return matmul(smat[number], hi) + matmul(smat[number], lo)
+    def gather(part, sections):
+        flux = jnp.zeros((rows, width), F32)
+        for a in sections:
+            pltpu.make_async_copy(recv.at[part, a], recv.at[part, a], fr_sem.at[part, a]).wait()
+            hi, lo = split(recv[part, a].reshape(n_tile * cap, width))
+            flux = flux + matmul(smat[a], hi) + matmul(smat[a], lo)
+        return flux
 
     def give_back():
         ocean_tile = flipped(tile)
 
         def one(k, c):
             i = lax.rem(k, 16)
-            j = i // 2
-            z = 2 * (k // 16) + lax.rem(i + tile // 8, 2)
-            t = 8 * z + 2 * lax.rem(j + tile // 2, 4) + j // 4
-
-            def to(a):
+            z = 2 * (k // 16) + lax.rem(i // 4 + tile // 8, 2)
+            t = 8 * z + 2 * lax.rem(i + tile // 2, 4) + i // 8
+
+            z2 = 2 * (k // 16) + lax.rem(i // 8 + tile // 8, 2)
+            t2 = 8 * z2 + 2 * lax.rem(i // 2 + tile // 2, 4) + lax.rem(i, 2)
+
+            def to(a, t):
                 return pltpu.make_async_remote_copy(
                     src_ref=ret.at[a * n_tile + lax.rem(t, 2) * half + t // 2],
                     dst_ref=arr.at[ocean_tile],
@@ -343,11 +410,10 @@
 
             @pl.when(t != tile)
             def _():
-                to(relay_sec).start()
-
-            for a in range(n_atm):
-                if a != relay_sec:
-                    to(a).start()
+                to(relay_sec, t).start()
+
+            to(0, t).start()
+            to(near_sec, t2).start()
             return c
 
         lax.fori_loop(0, n_tile, one, 0)
@@ -355,43 +421,42 @@
             ret.at[relay_sec * n_tile + parity * half + tile // 2], arr.at[ocean_tile], br_sem
         ).start()
 
-    def partial_copy():
-        return pltpu.make_async_remote_copy(
-            src_ref=mine_sum,
-            dst_ref=far_sum.at[sec],
-            send_sem=ps_sem,
-            recv_sem=pr_sem.at[sec],
-            device_id=(ocean_sec, flipped(tile)),
-            device_id_type=pl.DeviceIdType.MESH,
-        )
-
     @pl.when(jnp.logical_not(is_ocean))
     def _():
         pack(0, fo[0, 0])
-        pl.semaphore_wait(z_sem, n_tile // 2 - 1)
-
-        @pl.when(is_relay)
-        def _():
-            ship(0, relay_sec, False)
 
         @pl.when(jnp.logical_not(is_relay))
         def _():
-            ship(0, relay_sec, True)
-
+            pl.semaphore_wait(k_sem, 1)
+
+        ship(0, relay_sec)
         for l in range(1, levels):
             fo[0, l] = stencil(l)
         pack(1, fo[0, 0] - fo[0, 1])
 
+
+        @pl.when(jnp.logical_not(is_relay))
+        def _():
+            shipped(0, 0)
+
+        @pl.when(is_relay)
+        def _():
+            shipped(0, 1)
+
         @pl.when(is_near)
         def _():
-            ship(1, ocean_sec, True)
-
-        for a in range(near_sec):
-
-            @pl.when(sec == a)
+            pl.semaphore_wait(o_sem, 1)
+            ship(1, ocean_sec)
+
+        @pl.when(sec < near_sec)
+        def _():
+            pl.semaphore_wait(b_sem, 1)
+
+            @pl.when(is_relay)
             def _():
-                ship(1, a, False)
-
+                greet(b_sem, 0, tile)
+
+            ship(1, ocean_sec)
 
         for t in range(ntab):
             hi, lo = split(tab[t].T)
@@ -403,9 +468,7 @@
             mask_copy().wait_recv()
             base_copy().wait_recv()
             water = far_mask[...].astype(F32)
-            flux = spread(near_sec, 0, near_sec)
-            for a in (1, 0):
-                flux = flux + spread(a, 0, a)
+            flux = gather(0, (1, 0, 2))
             flux0[...] = flux
             flux_copy().start()
             hi, lo = split(water * (base[...] + forcing_rate * water * flux))
@@ -413,11 +476,6 @@
             for a in range(n_atm):
                 ret[a * n_tile : (a + 1) * n_tile] = matmul(rmat[a], both).reshape(n_tile, cap, width)
             give_back()
-
-        @pl.when(is_far)
-        def _():
-            mine_sum[...] = spread(sec, 1, sec)
-            partial_copy().start()
 
         pltpu.make_async_copy(arr, arr, br_sem).wait()
         uhi, ulo = split(arr[...].reshape(n_tile * cap, width))
@@ -429,44 +487,26 @@
             total = total + r[:rows] + r[rows:] + matmul(vhi, ttlo[t])
         su[0] = total
 
+        shipped(1, 0)
+
         @pl.when(is_relay)
         def _():
-            shipped(0, False)
             others = ret.at[1 : n_atm * n_tile]
             pltpu.make_async_copy(others, others, bs_sem).wait()
             flux_copy().wait_send()
 
-        @pl.when(jnp.logical_not(is_relay))
-        def _():
-            shipped(0, True)
-
-        @pl.when(is_near)
-        def _():
-            shipped(1, True)
-
-        @pl.when(is_far)
-        def _():
-            shipped(1, False)
-            partial_copy().wait_send()
-
-
     @pl.when(is_ocean)
     def _():
         base[...] = fo[0, 0]
         base_copy().start()
-        pl.semaphore_wait(z_sem, n_tile // 2 - 1)
         for l in range(1, levels):
             fo[0, l] = stencil(l)
         water = mask[...].astype(F32)
-        flux = spread(near_sec, 1, near_sec)
-        for a in range(near_sec):
-            pltpu.make_async_copy(far_sum.at[a], far_sum.at[a], pr_sem.at[a]).wait()
-            flux = flux + far_sum[a]
-        fo[0, 1] = fo[0, 1] + forcing_rate * water * flux
         flux_copy().wait_recv()
         first = fo[0, 0] + forcing_rate * water * flux0[...]
         fo[0, 0] = first
         su[0] = water * first
+        fo[0, 1] = fo[0, 1] + forcing_rate * water * gather(1, (2, 1, 0))
         mask_copy().wait_send()
         base_copy().wait_send()
 
@@ -522,8 +562,6 @@
         pltpu.VMEM((n_atm * n_tile, cap, width), F32),
         pltpu.VMEM((n_tile, cap, width), F32),
         pltpu.VMEM((rows, width), F32),
-        pltpu.VMEM((n_atm - 1, rows, width), F32),
-        pltpu.VMEM((rows, width), F32),
         pltpu.VMEM((rows, width), F32),
         pltpu.VMEM((rows, width), jnp.int32),
         pltpu.SemaphoreType.DMA((7,)),
@@ -533,8 +571,9 @@
         pltpu.SemaphoreType.DMA((2, n_atm)),
         pltpu.SemaphoreType.DMA,
         pltpu.SemaphoreType.DMA,
-        pltpu.SemaphoreType.DMA,
-        pltpu.SemaphoreType.DMA((n_atm - 1,)),
+        pltpu.SemaphoreType.REGULAR,
+        pltpu.SemaphoreType.REGULAR,
+        pltpu.SemaphoreType.REGULAR,
         pltpu.SemaphoreType.REGULAR,
         pltpu.SemaphoreType.DMA((3,)),
         pltpu.SemaphoreType.DMA((3,)),

time: 29.4 us -> 26.5 us (0.901)
  Pallas kernels: 28.6 us -> 25.7 us
    pallas_call x1, Pallas kernels: 27.9 us -> 25 us  [local(): pl.pallas_call(functools.partial(kernel, n_sec, n_tile, cap), out_shape=s...]
where the time goes in v5:
time: 26.5 us; the launch traced here: 26.4 us
  Pallas kernels  25.7 us (97%)
  between operations  0.64 us (2%)
    pallas_call x1, Pallas kernels, local(): pl.pallas_call(functools.partial(kernel, n_sec, n_tile, cap), out_shape=s...  25 us
    pallas_call x1, Pallas kernels, local(): pl.pallas_call(store, out_shape=shapes, in_specs=[pl.BlockSpec(memory_spa...  0.74 us

profile of v5, /device:TPU:1, one launch (start us, length us, event | category | flops | bytes accessed | tf_op | source)
XLA Modules:
  0.0 26.4 jit_solution(3047801589532507589)
XLA Ops:
  0.6 25.0 %shard_map.86 = (f32[1,4,64,256]{3,2,1,0:T(8,128)S(1)}, f32[1,64,256]{2,1,0:T(8,128)S(1)}) custom-call(f32[1,4,64,256]{3,2,1,0:T(8,128)} %fields.1, f32[1,2,64,256]{3,2,1,0:T(8,128)} %coef.1, s32[2,6144]{1,0:T(2,128)} %bitcast.3, s32[2,6144]{1,0:T(2,128)} %bitcast.4, s32[2,6144]{1,0:T(2,128)} %bitcast.5, f32[4,256,256]{2,1,0:T(8,128)} %tables.1, ...), custom_call_target="tpu_custom_call" | custom-call | tf_op jit(solution)/shard_map/pallas_call | solution.py:586
  25.6 0.7 %shard_map.87 = (f32[1,4,64,256]{3,2,1,0:T(8,128)}, f32[1,64,256]{2,1,0:T(8,128)}) custom-call(f32[1,4,64,256]{3,2,1,0:T(8,128)S(1)} %get-tuple-element.4.fields, f32[1,64,256]{2,1,0:T(8,128)S(1)} %get-tuple-element.5.surface), custom_call_target="tpu_custom_call" | custom-call | tf_op jit(solution)/shard_map/pallas_call | solution.py:599

commit v6 on v5

--- a/solution.py
+++ b/solution.py
@@ -12,6 +12,7 @@
 F32 = jnp.float32
 BF16 = jnp.bfloat16
 PAD = 8
+PLANES = 4
 
 
 def matmul(a, b):
@@ -33,14 +34,16 @@
     fo, su,
     ext, cext, ot, db, ti, tab, mask, hsend, hrecv,
     thi, tlo, tthi, ttlo, mmat, mtmat, pthi, ptlo, send, recv,
-    x0, x1, d0, d1, smat, rmat, ret, arr, base, flux0, far_mask,
-    in_sem, hs_sem, hr_sem, fs_sem, fr_sem, bs_sem, br_sem, o_sem, p_sem, k_sem, b_sem, cs_sem, cr_sem,
+    x0, x1, d0, d1, hots, smat, rmat, ret, arr, base, flux0, far_mask,
+    in_sem, hs_sem, hr_sem, fs_sem, fr_sem, bs_sem, br_sem, o_sem, p_sem, k_sem, g_sem, h_sem, cs_sem, cr_sem,
 ):
     n_atm = n_sec - 1
     ocean_sec = n_sec - 1
     near_sec = n_sec - 2
     relay_sec = near_sec - 1
     half = n_tile // 2
+    in_plane = n_tile // PLANES // 2
+    filled = n_atm * in_plane
     levels, rows, width = fo.shape[1:]
     ntab = tables.shape[0]
     top, low = PAD, PAD + rows
@@ -87,6 +90,19 @@
     def _():
         hrecv[1] = jnp.zeros_like(hrecv[1])
 
+    def clear(part):
+        for z in range(PLANES):
+            for h in range(2):
+                recv[part, z, h, filled:] = jnp.zeros_like(recv[part, z, h, filled:])
+
+    @pl.when(is_relay)
+    def _():
+        clear(0)
+
+    @pl.when(is_ocean)
+    def _():
+        clear(1)
+
     @pl.when(has_upper)
     def _():
         greet(barrier, sec, upper)
@@ -95,27 +111,26 @@
     def _():
         greet(barrier, sec, lower)
 
-    @pl.when(is_relay | is_ocean)
-    def _():
+    def greet_plane(semaphore):
         def one(k, c):
             z = lax.rem(tile // 8 + k // 4, 4)
             x = lax.rem(tile // 2 + lax.rem(k, 4), 4)
-            greet(barrier, sec, z * 8 + x * 2 + parity)
+            greet(semaphore, sec, z * 8 + x * 2 + parity)
             return c
 
         lax.fori_loop(1, half, one, 0)
 
     @pl.when(is_relay)
     def _():
+        greet_plane(barrier)
         greet(barrier, ocean_sec, flipped(tile))
 
     @pl.when(sec == 0)
     def _():
         greet(barrier, relay_sec, tile)
 
-    @pl.when(is_near)
-    def _():
-        greet(barrier, ocean_sec, tile)
+    @pl.when(is_near | is_ocean)
+    def _():
         greet(barrier, relay_sec, flipped(tile))
 
     zero = jnp.zeros((PAD, width), F32)
@@ -136,9 +151,13 @@
         hsend[0, 8 + c : 9 + c, :] = cext[c, top : top + 1, :]
         hsend[1, 8 + c : 9 + c, :] = cext[c, low - 1 : low, :]
 
-    @pl.when(is_relay | is_ocean)
-    def _():
-        pl.semaphore_wait(barrier, neighbours + half + 1)
+    @pl.when(is_relay)
+    def _():
+        pl.semaphore_wait(barrier, neighbours + half + 2)
+
+    @pl.when(is_ocean)
+    def _():
+        pl.semaphore_wait(barrier, neighbours + 1)
 
     @pl.when(jnp.logical_not(is_relay | is_ocean))
     def _():
@@ -188,9 +207,10 @@
         loads[6].wait()
         mask_copy().start()
 
-    @pl.when(is_relay | is_ocean)
+    @pl.when(is_relay)
     def _():
         greet(p_sem, sec, flipped(tile))
+        greet_plane(g_sem)
 
     loads[2].wait()
     loads[3].wait()
@@ -236,22 +256,21 @@
         left_c = lane_c < 64
         want = (lax.rem(lane_c, 64) + 1).astype(F32)
         hot = (matmul(named, both) == want).astype(F32)
-        turned = hot.T
-        smat[number, :, 0:count] = turned[0:64].astype(BF16)
-        smat[number, :, count : 2 * count] = turned[64:128].astype(BF16)
+        width_z = in_plane * cap
+        for z in range(PLANES):
+            hots[z, a * width_z : (a + 1) * width_z, :] = hot[z * width_z : (z + 1) * width_z]
         other = pltpu.roll(hot, 64, 1)
         rmat[number, 0:count, :] = jnp.where(left_c, hot, other).astype(BF16)
         rmat[number, count : 2 * count, :] = jnp.where(left_c, other, hot).astype(BF16)
 
-    @pl.when(is_ocean)
-    def _():
+    def place_all(owner):
+        hots[:, filled * cap :, :] = jnp.zeros_like(hots[:, filled * cap :, :])
         for a in range(n_atm):
-            place(a, a, tile)
-
-    @pl.when(is_relay)
-    def _():
-        for a in range(n_atm):
-            place(a, a, flipped(tile))
+            place(a, a, owner)
+        for z in range(PLANES):
+            turned = hots[z].T
+            smat[z, :, 0:128] = turned[0:64].astype(BF16)
+            smat[z, :, 128:256] = turned[64:128].astype(BF16)
 
     @pl.when(jnp.logical_not(is_ocean))
     def _():
@@ -296,11 +315,10 @@
         greet(k_sem, 0, tile)
         greet(k_sem, near_sec, flipped(tile))
 
-    @pl.when(is_ocean)
-    def _():
-        pl.semaphore_wait(p_sem, 1)
-        greet(o_sem, near_sec, tile)
-        greet(b_sem, relay_sec, flipped(tile))
+    @pl.when(is_relay)
+    def _():
+        pl.semaphore_wait(g_sem, half - 1)
+        greet(h_sem, sec, flipped(tile))
 
     @pl.when(has_upper)
     def _():
@@ -350,9 +368,9 @@
             t = lax.rem(tile + k, n_tile)
             pltpu.make_async_remote_copy(
                 src_ref=send.at[part, t if to == ocean_sec else flipped(t)],
-                dst_ref=recv.at[part, sec, parity, tile // 2],
+                dst_ref=recv.at[part, tile // 8, parity, sec * in_plane + lax.rem(tile // 2, in_plane)],
                 send_sem=fs_sem.at[part],
-                recv_sem=fr_sem.at[part, sec],
+                recv_sem=fr_sem.at[part, tile // 8],
                 device_id=(to, t),
                 device_id_type=pl.DeviceIdType.MESH,
             ).start()
@@ -366,8 +384,8 @@
         def _():
             pltpu.make_async_copy(
                 send.at[part, flipped(tile)],
-                recv.at[part, sec, parity, tile // 2],
-                fr_sem.at[part, sec],
+                recv.at[part, tile // 8, parity, sec * in_plane + lax.rem(tile // 2, in_plane)],
+                fr_sem.at[part, tile // 8],
             ).start()
             lax.fori_loop(1, n_tile, one, 0)
 
@@ -379,15 +397,16 @@
         sent = send.at[part, kept:n_tile]
         pltpu.make_async_copy(sent, sent, fs_sem.at[part]).wait()
 
-    def gather(part, sections):
+    def gather(part):
         flux = jnp.zeros((rows, width), F32)
-        for a in sections:
-            pltpu.make_async_copy(recv.at[part, a], recv.at[part, a], fr_sem.at[part, a]).wait()
-            hi, lo = split(recv[part, a].reshape(n_tile * cap, width))
-            flux = flux + matmul(smat[a], hi) + matmul(smat[a], lo)
+        for z in range(PLANES):
+            came = recv.at[part, z, :, 0:filled]
+            pltpu.make_async_copy(came, came, fr_sem.at[part, z]).wait()
+            hi, lo = split(recv[part, z].reshape(4 * rows, width))
+            flux = flux + matmul(smat[z], hi) + matmul(smat[z], lo)
         return flux
 
-    def give_back():
+    def give_back(first_k, last_k):
         ocean_tile = flipped(tile)
 
         def one(k, c):
@@ -416,7 +435,10 @@
             to(near_sec, t2).start()
             return c
 
-        lax.fori_loop(0, n_tile, one, 0)
+        lax.fori_loop(first_k, last_k, one, 0)
+
+    def keep_own():
+        ocean_tile = flipped(tile)
         pltpu.make_async_copy(
             ret.at[relay_sec * n_tile + parity * half + tile // 2], arr.at[ocean_tile], br_sem
         ).start()
@@ -430,6 +452,13 @@
             pl.semaphore_wait(k_sem, 1)
 
         ship(0, relay_sec)
+
+        @pl.when(is_relay)
+        def _():
+            pl.semaphore_wait(h_sem, 1)
+            greet(o_sem, 0, tile)
+            greet(o_sem, near_sec, flipped(tile))
+
         for l in range(1, levels):
             fo[0, l] = stencil(l)
         pack(1, fo[0, 0] - fo[0, 1])
@@ -443,20 +472,15 @@
         def _():
             shipped(0, 1)
 
-        @pl.when(is_near)
+        @pl.when(jnp.logical_not(is_relay))
         def _():
             pl.semaphore_wait(o_sem, 1)
-            ship(1, ocean_sec)
-
-        @pl.when(sec < near_sec)
-        def _():
-            pl.semaphore_wait(b_sem, 1)
-
-            @pl.when(is_relay)
-            def _():
-                greet(b_sem, 0, tile)
-
-            ship(1, ocean_sec)
+
+        ship(1, ocean_sec)
+
+        @pl.when(is_relay)
+        def _():
+            place_all(flipped(tile))
 
         for t in range(ntab):
             hi, lo = split(tab[t].T)
@@ -468,14 +492,21 @@
             mask_copy().wait_recv()
             base_copy().wait_recv()
             water = far_mask[...].astype(F32)
-            flux = gather(0, (1, 0, 2))
+            flux = gather(0)
             flux0[...] = flux
             flux_copy().start()
             hi, lo = split(water * (base[...] + forcing_rate * water * flux))
             both = jnp.concatenate([hi, lo], axis=0)
-            for a in range(n_atm):
-                ret[a * n_tile : (a + 1) * n_tile] = matmul(rmat[a], both).reshape(n_tile, cap, width)
-            give_back()
+            count = half * cap // 2
+            for low_high in range(2):
+                for a in range(n_atm):
+                    for h in range(2):
+                        n = 2 * h + low_high
+                        ret[a * n_tile + n * 8 : a * n_tile + n * 8 + 8] = matmul(
+                            rmat[a, n * count : (n + 1) * count], both
+                        ).reshape(8, cap, width)
+                give_back(low_high * half, (low_high + 1) * half)
+            keep_own()
 
         pltpu.make_async_copy(arr, arr, br_sem).wait()
         uhi, ulo = split(arr[...].reshape(n_tile * cap, width))
@@ -499,6 +530,7 @@
     def _():
         base[...] = fo[0, 0]
         base_copy().start()
+        place_all(tile)
         for l in range(1, levels):
             fo[0, l] = stencil(l)
         water = mask[...].astype(F32)
@@ -506,7 +538,7 @@
         first = fo[0, 0] + forcing_rate * water * flux0[...]
         fo[0, 0] = first
         su[0] = water * first
-        fo[0, 1] = fo[0, 1] + forcing_rate * water * gather(1, (2, 1, 0))
+        fo[0, 1] = fo[0, 1] + forcing_rate * water * gather(1)
         mask_copy().wait_send()
         base_copy().wait_send()
 
@@ -552,12 +584,13 @@
         pltpu.VMEM((ntab * rows, width), BF16),
         pltpu.VMEM((ntab * rows, width), BF16),
         pltpu.VMEM((2, n_tile, cap, width), F32),
-        pltpu.VMEM((2, n_atm, 2, half, cap, width), F32),
+        pltpu.VMEM((2, PLANES, 2, 16, cap, width), F32),
         pltpu.VMEM((half, 2 * rows), F32),
         pltpu.VMEM((half, 2 * rows), F32),
         pltpu.VMEM((half, 2 * rows), F32),
         pltpu.VMEM((half, 2 * rows), F32),
-        pltpu.VMEM((n_atm, rows, slots), BF16),
+        pltpu.VMEM((PLANES, 2 * rows, 2 * rows), F32),
+        pltpu.VMEM((PLANES, rows, 4 * rows), BF16),
         pltpu.VMEM((n_atm, slots, 2 * rows), BF16),
         pltpu.VMEM((n_atm * n_tile, cap, width), F32),
         pltpu.VMEM((n_tile, cap, width), F32),
@@ -568,9 +601,10 @@
         pltpu.SemaphoreType.DMA((2,)),
         pltpu.SemaphoreType.DMA((2,)),
         pltpu.SemaphoreType.DMA((2,)),
-        pltpu.SemaphoreType.DMA((2, n_atm)),
+        pltpu.SemaphoreType.DMA((2, PLANES)),
         pltpu.SemaphoreType.DMA,
         pltpu.SemaphoreType.DMA,
+        pltpu.SemaphoreType.REGULAR,
         pltpu.SemaphoreType.REGULAR,
         pltpu.SemaphoreType.REGULAR,
         pltpu.SemaphoreType.REGULAR,

time: 26.5 us -> 26.5 us (level)
  no operation moved by 1% of the time
where the time goes in v6:
time: 26.5 us; the launch traced here: 26.3 us
  Pallas kernels  25.7 us (97%)
  between operations  0.64 us (2%)
    pallas_call x1, Pallas kernels, local(): pl.pallas_call(functools.partial(kernel, n_sec, n_tile, cap), out_shape=s...  25 us
    pallas_call x1, Pallas kernels, local(): pl.pallas_call(store, out_shape=shapes, in_specs=[pl.BlockSpec(memory_spa...  0.74 us

profile of v6, /device:TPU:1, one launch (start us, length us, event | category | flops | bytes accessed | tf_op | source)
XLA Modules:
  0.0 26.3 jit_solution(17580087534720320834)
XLA Ops:
  0.6 25.0 %shard_map.86 = (f32[1,4,64,256]{3,2,1,0:T(8,128)S(1)}, f32[1,64,256]{2,1,0:T(8,128)S(1)}) custom-call(f32[1,4,64,256]{3,2,1,0:T(8,128)} %fields.1, f32[1,2,64,256]{3,2,1,0:T(8,128)} %coef.1, s32[2,6144]{1,0:T(2,128)} %bitcast.3, s32[2,6144]{1,0:T(2,128)} %bitcast.4, s32[2,6144]{1,0:T(2,128)} %bitcast.5, f32[4,256,256]{2,1,0:T(8,128)} %tables.1, ...), custom_call_target="tpu_custom_call" | custom-call | tf_op jit(solution)/shard_map/pallas_call | solution.py:620
  25.6 0.7 %shard_map.87 = (f32[1,4,64,256]{3,2,1,0:T(8,128)}, f32[1,64,256]{2,1,0:T(8,128)}) custom-call(f32[1,4,64,256]{3,2,1,0:T(8,128)S(1)} %get-tuple-element.4.fields, f32[1,64,256]{2,1,0:T(8,128)S(1)} %get-tuple-element.5.surface), custom_call_target="tpu_custom_call" | custom-call | tf_op jit(solution)/shard_map/pallas_call | solution.py:633

commit v7 on v6

--- a/solution.py
+++ b/solution.py
@@ -412,7 +412,7 @@
         def one(k, c):
             i = lax.rem(k, 16)
             z = 2 * (k // 16) + lax.rem(i // 4 + tile // 8, 2)
-            t = 8 * z + 2 * lax.rem(i + tile // 2, 4) + i // 8
+            t = 8 * z + 2 * lax.rem(i, 4) + i // 8
 
             z2 = 2 * (k // 16) + lax.rem(i // 8 + tile // 8, 2)
             t2 = 8 * z2 + 2 * lax.rem(i // 2 + tile // 2, 4) + lax.rem(i, 2)

time: 26.5 us -> 26.1 us (0.985)
  Pallas kernels: 25.7 us -> 25.4 us
    pallas_call x1, Pallas kernels: 25 us -> 24.6 us  [local(): pl.pallas_call(functools.partial(kernel, n_sec, n_tile, cap), out_shape=s...]
where the time goes in v7:
time: 26.1 us; the launch traced here: 26 us
  Pallas kernels  25.4 us (97%)
  between operations  0.64 us (2%)
    pallas_call x1, Pallas kernels, local(): pl.pallas_call(functools.partial(kernel, n_sec, n_tile, cap), out_shape=s...  24.6 us
    pallas_call x1, Pallas kernels, local(): pl.pallas_call(store, out_shape=shapes, in_specs=[pl.BlockSpec(memory_spa...  0.74 us

profile of v7, /device:TPU:1, one launch (start us, length us, event | category | flops | bytes accessed | tf_op | source)
XLA Modules:
  0.0 26.0 jit_solution(10851088258093312379)
XLA Ops:
  0.6 24.6 %shard_map.86 = (f32[1,4,64,256]{3,2,1,0:T(8,128)S(1)}, f32[1,64,256]{2,1,0:T(8,128)S(1)}) custom-call(f32[1,4,64,256]{3,2,1,0:T(8,128)} %fields.1, f32[1,2,64,256]{3,2,1,0:T(8,128)} %coef.1, s32[2,6144]{1,0:T(2,128)} %bitcast.3, s32[2,6144]{1,0:T(2,128)} %bitcast.4, s32[2,6144]{1,0:T(2,128)} %bitcast.5, f32[4,256,256]{2,1,0:T(8,128)} %tables.1, ...), custom_call_target="tpu_custom_call" | custom-call | tf_op jit(solution)/shard_map/pallas_call | solution.py:620
  25.3 0.7 %shard_map.87 = (f32[1,4,64,256]{3,2,1,0:T(8,128)}, f32[1,64,256]{2,1,0:T(8,128)}) custom-call(f32[1,4,64,256]{3,2,1,0:T(8,128)S(1)} %get-tuple-element.4.fields, f32[1,64,256]{2,1,0:T(8,128)S(1)} %get-tuple-element.5.surface), custom_call_target="tpu_custom_call" | custom-call | tf_op jit(solution)/shard_map/pallas_call | solution.py:633

commit v8 on v7

--- a/solution.py
+++ b/solution.py
@@ -140,16 +140,18 @@
     for c in range(2):
         cext[c, 0:top, :] = zero
         cext[c, low : low + PAD, :] = zero
-        hsend[c, 8:16, :] = zero
+        hsend[c, 0] = zero
+        hsend[c, 1] = zero
 
     loads[0].wait()
     for l in range(levels):
-        hsend[0, 2 * l : 2 * l + 2, :] = ext[l, top : top + 2, :]
-        hsend[1, 2 * l : 2 * l + 2, :] = ext[l, low - 2 : low, :]
+        group, at = (0, 0) if l == 0 else (1, 2 * l - 2)
+        hsend[0, group, at : at + 2, :] = ext[l, top : top + 2, :]
+        hsend[1, group, at : at + 2, :] = ext[l, low - 2 : low, :]
     loads[1].wait()
     for c in range(2):
-        hsend[0, 8 + c : 9 + c, :] = cext[c, top : top + 1, :]
-        hsend[1, 8 + c : 9 + c, :] = cext[c, low - 1 : low, :]
+        hsend[0, 0, 2 + c : 3 + c, :] = cext[c, top : top + 1, :]
+        hsend[1, 0, 2 + c : 3 + c, :] = cext[c, low - 1 : low, :]
 
     @pl.when(is_relay)
     def _():
@@ -182,25 +184,36 @@
     def flux_copy():
         return column_copy(flux0, flux0, 2, ocean_sec)
 
-    def halo(way, to):
+    def halo(way, to, group):
         return pltpu.make_async_remote_copy(
-            src_ref=hsend.at[way],
-            dst_ref=hrecv.at[1 - way],
-            send_sem=hs_sem.at[way],
-            recv_sem=hr_sem.at[1 - way],
+            src_ref=hsend.at[way, group],
+            dst_ref=hrecv.at[1 - way, group],
+            send_sem=hs_sem.at[way, group],
+            recv_sem=hr_sem.at[1 - way, group],
             device_id=(sec, to),
             device_id_type=pl.DeviceIdType.MESH,
         )
 
-    halos = [halo(0, upper), halo(1, lower)]
-
-    @pl.when(has_upper)
-    def _():
-        halos[0].start()
-
-    @pl.when(has_lower)
-    def _():
-        halos[1].start()
+    for group in range(2):
+
+        @pl.when(has_upper)
+        def _():
+            halo(0, upper, group).start()
+
+        @pl.when(has_lower)
+        def _():
+            halo(1, lower, group).start()
+
+    def halo_wait(group):
+        @pl.when(has_upper)
+        def _():
+            halo(0, upper, group).wait_send()
+            halo(1, lower, group).wait_recv()
+
+        @pl.when(has_lower)
+        def _():
+            halo(1, lower, group).wait_send()
+            halo(0, upper, group).wait_recv()
 
     @pl.when(is_ocean)
     def _():
@@ -320,23 +333,21 @@
         pl.semaphore_wait(g_sem, half - 1)
         greet(h_sem, sec, flipped(tile))
 
-    @pl.when(has_upper)
-    def _():
-        halos[0].wait_send()
-        halos[1].wait_recv()
-
-    @pl.when(has_lower)
-    def _():
-        halos[1].wait_send()
-        halos[0].wait_recv()
-
-    above, below = hrecv[0], hrecv[1]
-    for l in range(levels):
-        ext[l, top - 2 : top, :] = above[2 * l : 2 * l + 2]
-        ext[l, low : low + 2, :] = below[2 * l : 2 * l + 2]
+    halo_wait(0)
+    above, below = hrecv[0, 0], hrecv[1, 0]
+    ext[0, top - 2 : top, :] = above[0:2]
+    ext[0, low : low + 2, :] = below[0:2]
     for c in range(2):
-        cext[c, top - 1 : top, :] = above[8 + c : 9 + c]
-        cext[c, low : low + 1, :] = below[8 + c : 9 + c]
+        cext[c, top - 1 : top, :] = above[2 + c : 3 + c]
+        cext[c, low : low + 1, :] = below[2 + c : 3 + c]
+
+    def other_levels():
+        halo_wait(1)
+        above, below = hrecv[0, 1], hrecv[1, 1]
+        for l in range(1, levels):
+            ext[l, top - 2 : top, :] = above[2 * l - 2 : 2 * l]
+            ext[l, low : low + 2, :] = below[2 * l - 2 : 2 * l]
+            fo[0, l] = stencil(l)
 
     def substep(u, kappa, speed):
         n = u.shape[0]
@@ -459,8 +470,7 @@
             greet(o_sem, 0, tile)
             greet(o_sem, near_sec, flipped(tile))
 
-        for l in range(1, levels):
-            fo[0, l] = stencil(l)
+        other_levels()
         pack(1, fo[0, 0] - fo[0, 1])
 
 
@@ -531,8 +541,7 @@
         base[...] = fo[0, 0]
         base_copy().start()
         place_all(tile)
-        for l in range(1, levels):
-            fo[0, l] = stencil(l)
+        other_levels()
         water = mask[...].astype(F32)
         flux_copy().wait_recv()
         first = fo[0, 0] + forcing_rate * water * flux0[...]
@@ -573,8 +582,8 @@
         pltpu.VMEM((fan_out, blocks), jnp.int32),
         pltpu.VMEM((ntab, width, width), F32),
         pltpu.VMEM((rows, width), jnp.int32),
-        pltpu.VMEM((2, 16, width), F32),
-        pltpu.VMEM((2, 16, width), F32),
+        pltpu.VMEM((2, 2, 8, width), F32),
+        pltpu.VMEM((2, 2, 8, width), F32),
         pltpu.VMEM((ntab, width, width), BF16),
         pltpu.VMEM((ntab, width, width), BF16),
         pltpu.VMEM((ntab, width, width), BF16),
@@ -598,8 +607,8 @@
         pltpu.VMEM((rows, width), F32),
         pltpu.VMEM((rows, width), jnp.int32),
         pltpu.SemaphoreType.DMA((7,)),
-        pltpu.SemaphoreType.DMA((2,)),
-        pltpu.SemaphoreType.DMA((2,)),
+        pltpu.SemaphoreType.DMA((2, 2)),
+        pltpu.SemaphoreType.DMA((2, 2)),
         pltpu.SemaphoreType.DMA((2,)),
         pltpu.SemaphoreType.DMA((2, PLANES)),
         pltpu.SemaphoreType.DMA,

time: 26.1 us -> 26.1 us (level)
  no operation moved by 1% of the time
where the time goes in v8:
time: 26.1 us; the launch traced here: 25.9 us
  Pallas kernels  25.3 us (97%)
  between operations  0.64 us (2%)
    pallas_call x1, Pallas kernels, local(): pl.pallas_call(functools.partial(kernel, n_sec, n_tile, cap), out_shape=s...  24.5 us
    pallas_call x1, Pallas kernels, local(): pl.pallas_call(store, out_shape=shapes, in_specs=[pl.BlockSpec(memory_spa...  0.74 us

profile of v8, /device:TPU:1, one launch (start us, length us, event | category | flops | bytes accessed | tf_op | source)
XLA Modules:
  0.0 25.9 jit_solution(10670431644823195383)
XLA Ops:
  0.6 24.5 %shard_map.86 = (f32[1,4,64,256]{3,2,1,0:T(8,128)S(1)}, f32[1,64,256]{2,1,0:T(8,128)S(1)}) custom-call(f32[1,4,64,256]{3,2,1,0:T(8,128)} %fields.1, f32[1,2,64,256]{3,2,1,0:T(8,128)} %coef.1, s32[2,6144]{1,0:T(2,128)} %bitcast.3, s32[2,6144]{1,0:T(2,128)} %bitcast.4, s32[2,6144]{1,0:T(2,128)} %bitcast.5, f32[4,256,256]{2,1,0:T(8,128)} %tables.1, ...), custom_call_target="tpu_custom_call" | custom-call | tf_op jit(solution)/shard_map/pallas_call | solution.py:629
  25.2 0.7 %shard_map.87 = (f32[1,4,64,256]{3,2,1,0:T(8,128)}, f32[1,64,256]{2,1,0:T(8,128)}) custom-call(f32[1,4,64,256]{3,2,1,0:T(8,128)S(1)} %get-tuple-element.4.fields, f32[1,64,256]{2,1,0:T(8,128)S(1)} %get-tuple-element.5.surface), custom_call_target="tpu_custom_call" | custom-call | tf_op jit(solution)/shard_map/pallas_call | solution.py:642

commit v9 on v8

--- a/solution.py
+++ b/solution.py
@@ -60,6 +60,51 @@
         return t + 1 - 2 * lax.rem(t, 2)
 
 
+    barrier = pltpu.get_barrier_semaphore()
+    has_upper, has_lower = tile > 0, tile < n_tile - 1
+    neighbours = has_upper.astype(jnp.int32) + has_lower.astype(jnp.int32)
+
+    def greet(semaphore, s, t):
+        pl.semaphore_signal(semaphore, inc=1, device_id=(s, t), device_id_type=pl.DeviceIdType.MESH)
+
+    @pl.when(jnp.logical_not(has_upper))
+    def _():
+        hrecv[0] = jnp.zeros_like(hrecv[0])
+
+    @pl.when(jnp.logical_not(has_lower))
+    def _():
+        hrecv[1] = jnp.zeros_like(hrecv[1])
+
+    @pl.when(has_upper)
+    def _():
+        greet(barrier, sec, upper)
+
+    @pl.when(has_lower)
+    def _():
+        greet(barrier, sec, lower)
+
+    def greet_plane(semaphore):
+        def one(k, c):
+            z = lax.rem(tile // 8 + k // 4, 4)
+            x = lax.rem(tile // 2 + lax.rem(k, 4), 4)
+            greet(semaphore, sec, z * 8 + x * 2 + parity)
+            return c
+
+        lax.fori_loop(1, half, one, 0)
+
+    @pl.when(is_relay)
+    def _():
+        greet_plane(barrier)
+        greet(barrier, ocean_sec, flipped(tile))
+
+    @pl.when(sec == 0)
+    def _():
+        greet(barrier, relay_sec, tile)
+
+    @pl.when(is_near | is_ocean)
+    def _():
+        greet(barrier, relay_sec, flipped(tile))
+
     def load(number, src, dst):
         return pltpu.make_async_copy(src, dst, in_sem.at[number])
 
@@ -75,21 +120,6 @@
     for copy in loads:
         copy.start()
 
-    barrier = pltpu.get_barrier_semaphore()
-    has_upper, has_lower = tile > 0, tile < n_tile - 1
-    neighbours = has_upper.astype(jnp.int32) + has_lower.astype(jnp.int32)
-
-    def greet(semaphore, s, t):
-        pl.semaphore_signal(semaphore, inc=1, device_id=(s, t), device_id_type=pl.DeviceIdType.MESH)
-
-    @pl.when(jnp.logical_not(has_upper))
-    def _():
-        hrecv[0] = jnp.zeros_like(hrecv[0])
-
-    @pl.when(jnp.logical_not(has_lower))
-    def _():
-        hrecv[1] = jnp.zeros_like(hrecv[1])
-
     def clear(part):
         for z in range(PLANES):
             for h in range(2):
@@ -102,36 +132,6 @@
     @pl.when(is_ocean)
     def _():
         clear(1)
-
-    @pl.when(has_upper)
-    def _():
-        greet(barrier, sec, upper)
-
-    @pl.when(has_lower)
-    def _():
-        greet(barrier, sec, lower)
-
-    def greet_plane(semaphore):
-        def one(k, c):
-            z = lax.rem(tile // 8 + k // 4, 4)
-            x = lax.rem(tile // 2 + lax.rem(k, 4), 4)
-            greet(semaphore, sec, z * 8 + x * 2 + parity)
-            return c
-
-        lax.fori_loop(1, half, one, 0)
-
-    @pl.when(is_relay)
-    def _():
-        greet_plane(barrier)
-        greet(barrier, ocean_sec, flipped(tile))
-
-    @pl.when(sec == 0)
-    def _():
-        greet(barrier, relay_sec, tile)
-
-    @pl.when(is_near | is_ocean)
-    def _():
-        greet(barrier, relay_sec, flipped(tile))
 
     zero = jnp.zeros((PAD, width), F32)
     for l in range(levels):

time: 26.1 us -> 26.1 us (level)
  no operation moved by 1% of the time
where the time goes in v9:
time: 26.1 us; the launch traced here: 25.9 us
  Pallas kernels  25.3 us (97%)
  between operations  0.64 us (2%)
    pallas_call x1, Pallas kernels, local(): pl.pallas_call(functools.partial(kernel, n_sec, n_tile, cap), out_shape=s...  24.5 us
    pallas_call x1, Pallas kernels, local(): pl.pallas_call(store, out_shape=shapes, in_specs=[pl.BlockSpec(memory_spa...  0.74 us

profile of v9, /device:TPU:1, one launch (start us, length us, event | category | flops | bytes accessed | tf_op | source)
XLA Modules:
  0.0 25.9 jit_solution(12264017698290391371)
XLA Ops:
  0.6 24.5 %shard_map.86 = (f32[1,4,64,256]{3,2,1,0:T(8,128)S(1)}, f32[1,64,256]{2,1,0:T(8,128)S(1)}) custom-call(f32[1,4,64,256]{3,2,1,0:T(8,128)} %fields.1, f32[1,2,64,256]{3,2,1,0:T(8,128)} %coef.1, s32[2,6144]{1,0:T(2,128)} %bitcast.3, s32[2,6144]{1,0:T(2,128)} %bitcast.4, s32[2,6144]{1,0:T(2,128)} %bitcast.5, f32[4,256,256]{2,1,0:T(8,128)} %tables.1, ...), custom_call_target="tpu_custom_call" | custom-call | tf_op jit(solution)/shard_map/pallas_call | solution.py:629
  25.2 0.7 %shard_map.87 = (f32[1,4,64,256]{3,2,1,0:T(8,128)}, f32[1,64,256]{2,1,0:T(8,128)}) custom-call(f32[1,4,64,256]{3,2,1,0:T(8,128)S(1)} %get-tuple-element.4.fields, f32[1,64,256]{2,1,0:T(8,128)S(1)} %get-tuple-element.5.surface), custom_call_target="tpu_custom_call" | custom-call | tf_op jit(solution)/shard_map/pallas_call | solution.py:642

commit v10 on v7

--- a/solution.py
+++ b/solution.py
@@ -259,9 +259,12 @@
         width_z = in_plane * cap
         for z in range(PLANES):
             hots[z, a * width_z : (a + 1) * width_z, :] = hot[z * width_z : (z + 1) * width_z]
-        other = pltpu.roll(hot, 64, 1)
-        rmat[number, 0:count, :] = jnp.where(left_c, hot, other).astype(BF16)
-        rmat[number, count : 2 * count, :] = jnp.where(left_c, other, hot).astype(BF16)
+
+        @pl.when(is_relay)
+        def _():
+            other = pltpu.roll(hot, 64, 1)
+            rmat[number, 0:count, :] = jnp.where(left_c, hot, other).astype(BF16)
+            rmat[number, count : 2 * count, :] = jnp.where(left_c, other, hot).astype(BF16)
 
     def place_all(owner):
         hots[:, filled * cap :, :] = jnp.zeros_like(hots[:, filled * cap :, :])

time: 26.1 us -> 26.1 us (level)
  no operation moved by 1% of the time
where the time goes in v10:
time: 26.1 us; the launch traced here: 26 us
  Pallas kernels  25.4 us (97%)
  between operations  0.64 us (2%)
    pallas_call x1, Pallas kernels, local(): pl.pallas_call(functools.partial(kernel, n_sec, n_tile, cap), out_shape=s...  24.6 us
    pallas_call x1, Pallas kernels, local(): pl.pallas_call(store, out_shape=shapes, in_specs=[pl.BlockSpec(memory_spa...  0.74 us

profile of v10, /device:TPU:1, one launch (start us, length us, event | category | flops | bytes accessed | tf_op | source)
XLA Modules:
  0.0 26.0 jit_solution(8854435554705363947)
XLA Ops:
  0.6 24.6 %shard_map.86 = (f32[1,4,64,256]{3,2,1,0:T(8,128)S(1)}, f32[1,64,256]{2,1,0:T(8,128)S(1)}) custom-call(f32[1,4,64,256]{3,2,1,0:T(8,128)} %fields.1, f32[1,2,64,256]{3,2,1,0:T(8,128)} %coef.1, s32[2,6144]{1,0:T(2,128)} %bitcast.3, s32[2,6144]{1,0:T(2,128)} %bitcast.4, s32[2,6144]{1,0:T(2,128)} %bitcast.5, f32[4,256,256]{2,1,0:T(8,128)} %tables.1, ...), custom_call_target="tpu_custom_call" | custom-call | tf_op jit(solution)/shard_map/pallas_call | solution.py:623
  25.3 0.7 %shard_map.87 = (f32[1,4,64,256]{3,2,1,0:T(8,128)}, f32[1,64,256]{2,1,0:T(8,128)}) custom-call(f32[1,4,64,256]{3,2,1,0:T(8,128)S(1)} %get-tuple-element.4.fields, f32[1,64,256]{2,1,0:T(8,128)S(1)} %get-tuple-element.5.surface), custom_call_target="tpu_custom_call" | custom-call | tf_op jit(solution)/shard_map/pallas_call | solution.py:636
